TPU v7x, 32 devices: a whole 2x2x4 slice. The times are simulated.
32 devices in a mesh: groups: 2 (over y), patch: 4 (over z), head: 4 (over x, core).
Axes of the slice: x: 2, y: 2, z: 4, core: 2. Of those that a mesh axis runs over, the one named last changes fastest.
Arguments:
- qkv: bfloat16 [1024, 3, 3072], P(('groups', 'patch', 'head')), parts along dimension 0, may hold values from -8 to 8
- stale_kv: bfloat16 [1024, 2, 3072], P(('groups', 'patch'), None, 'head'), parts along dimension 0, may hold values from -8 to 8
- w_out: bfloat16 [3072, 3072], P('head'), may hold values from -0.109375 to 0.109375
- gate_table: bfloat16 [50, 3072], replicated, may hold values from -4 to 4
- lengths: int32 [8], P('groups'), parts along dimension 0, may hold values from 1 to 96, 256 in all
- timestep: int32 [2], P('groups'), parts along dimension 0, may hold values from 0 to 49
Outputs:
- branch: bfloat16 [1024, 3072], P(('groups', 'patch', 'head')), parts along dimension 0
- next_kv: bfloat16 [1024, 2, 3072], P(('groups', 'patch'), None, 'head'), parts along dimension 0
There are 2 independent parts, one for each index of `groups`. A program takes and returns all parts, laid end to end along the dimension named above; an argument that names none is the same for every part. Nothing has to cross between parts.
Inputs may be any that keep to these rules, and one draw needn't show every extreme that they name: `lengths`: the live tokens are the first rows of each patch's 128 slots; no patch has more than 96 live tokens, and one has exactly 96.
All inputs are finite; a program needn't handle non-finite values.
Results may differ from a plain program's by a relative error of at most 0.013.
Values may be sent and summed in bfloat16 or wider, within the bound.
No kernel may reach another device: no remote copies, remote signals or barrier semaphores. Data moves between devices by JAX's collectives and lax.ppermute only.
A program may use at most 128 MiB of HBM per device.

v0:
```python
import math

import jax
import jax.numpy as jnp
from jax import lax
from jax.sharding import PartitionSpec as P

HEAD_DIM = 128


MASKED = -1e30


def attend_block(partial_value, queries, keys_here, values, usable, score_scale):
    running_max, weight_sum, weighted = partial_value
    scores = (
        jnp.einsum("qhe,khe->hqk", queries, keys_here, preferred_element_type=jnp.float32)
        * score_scale
    )
    scores = jnp.where(usable[None, None, :], scores, MASKED)
    new_max = jnp.maximum(running_max, jnp.max(scores, axis=2))
    weights = jnp.where(usable[None, None, :], jnp.exp(scores - new_max[:, :, None]), 0.0)
    shrink = jnp.exp(running_max - new_max)
    weight_sum = weight_sum * shrink + jnp.sum(weights, axis=2)
    weighted = weighted * shrink[:, :, None] + jnp.einsum(
        "hqk,khe->hqe", weights.astype(jnp.bfloat16), values, preferred_element_type=jnp.float32
    )
    return (new_max, weight_sum, weighted)


def fold_blocks(partial_value, stale_piece, queries, lengths, own_patch, row_stride, score_scale):
    row_count = stale_piece.shape[0]
    block_rows = math.gcd(row_count, 1024)
    heads_here = queries.shape[1]
    blocks = stale_piece.reshape(
        row_count // block_rows, block_rows, 2, heads_here, queries.shape[2]
    )
    patch_ids = lax.iota(jnp.int32, lengths.shape[0])

    def advance(state_now, element):
        kv_block, number = element
        positions = number * block_rows + lax.iota(jnp.int32, block_rows)
        owners = positions // row_stride
        within = positions - owners * row_stride
        matches = owners[:, None] == patch_ids[None, :]
        live_limit = jnp.sum(jnp.where(matches, lengths[None, :], 0), axis=1)
        usable = (within < live_limit) & (owners != own_patch)
        return (
            attend_block(state_now, queries, kv_block[:, 0], kv_block[:, 1], usable, score_scale),
            None,
        )

    numbers = lax.iota(jnp.int32, row_count // block_rows)
    partial_value, _ = lax.scan(advance, partial_value, (blocks, numbers))
    return partial_value


def shards(qkv, stale_kv, w_out, gate_table, lengths, timestep):
    heads_here = w_out.shape[0] // HEAD_DIM
    score_scale = 1.0 / math.sqrt(HEAD_DIM)
    regrouped = lax.all_to_all(qkv, "head", split_axis=2, concat_axis=0, tiled=True)
    patch_rows = regrouped.shape[0]
    queries = regrouped[:, 0].reshape(patch_rows, heads_here, HEAD_DIM)
    fresh_keys = regrouped[:, 1].reshape(patch_rows, heads_here, HEAD_DIM)
    fresh_values = regrouped[:, 2].reshape(patch_rows, heads_here, HEAD_DIM)
    next_kv = regrouped[:, 1:3]
    own_patch = lax.axis_index("patch")
    own_length = lax.dynamic_slice_in_dim(lengths, own_patch, 1, 0)[0]
    row_ids = lax.iota(jnp.int32, patch_rows)
    start_state = (
        jnp.full((heads_here, patch_rows), MASKED, jnp.float32),
        jnp.zeros((heads_here, patch_rows), jnp.float32),
        jnp.zeros((heads_here, patch_rows, HEAD_DIM), jnp.float32),
    )
    partial_value = attend_block(
        start_state, queries, fresh_keys, fresh_values, row_ids < own_length, score_scale
    )
    gathered = lax.all_gather(stale_kv, "patch", axis=0, tiled=True)
    partial_value = fold_blocks(
        partial_value, gathered, queries, lengths, own_patch, patch_rows, score_scale
    )
    running_max, weight_sum, weighted = partial_value
    mixed = weighted / weight_sum[:, :, None]
    attended = (
        jnp.transpose(mixed, (1, 0, 2))
        .reshape(patch_rows, heads_here * HEAD_DIM)
        .astype(jnp.bfloat16)
    )
    projected = lax.psum_scatter(
        jnp.dot(attended, w_out, preferred_element_type=jnp.float32).astype(jnp.bfloat16),
        "head",
        scatter_dimension=0,
        tiled=True,
    ).astype(jnp.float32)
    gate_row = lax.dynamic_slice_in_dim(gate_table, timestep[0], 1, 0)[0].astype(jnp.float32)
    branch = (gate_row[None, :] * projected).astype(jnp.bfloat16)
    return (branch, next_kv)


def solution(mesh):
    return jax.shard_map(
        shards,
        mesh=mesh,
        in_specs=(
            P(("groups", "patch", "head"), None, None),
            P(("groups", "patch"), None, "head"),
            P("head", None),
            P(),
            P("groups"),
            P("groups"),
        ),
        out_specs=(P(("groups", "patch", "head"), None), P(("groups", "patch"), None, "head")),
        check_vma=False,
    )
```

profile of v0, /device:TPU:0, one launch (start us, length us, event | category | flops | bytes accessed | tf_op | source)
XLA Modules:
  0.0 88.3 jit_solution(16408504691115877116)
XLA Ops:
  7.2 0.0 all-gather.2.cloned.1.call-start
  7.2 1.9 %copy.63 = bf16[128,2,768]{0,2,1:T(8,128)(2,1)} copy(bf16[128,2,768]{2,1,0:T(2,128)(2,1)} %param.7) | data formatting | bytes 786432 | tf_op args[1]
  9.1 0.0 all-gather.2.cloned.1.call-update
  9.2 4.5 %copy.54 = bf16[32,3,3072]{0,1,2:T(4,128)(2,1)S(1)} copy(bf16[32,3,3072]{2,0,1:T(8,128)(2,1)} %param.6) | data formatting | bytes 1179648 | tf_op args[0]
  13.6 0.0 copy-start.2
  13.6 3.1 %reshape.78 = bf16[4,2,36864]{2,1,0:T(2,128)(2,1)} reshape(bf16[3072,3,32]{2,1,0:T(4,128)(2,1)S(1)} %bitcast.69) | data formatting | bytes 1179648
  16.7 4.2 %all-to-all-start = ((bf16[4,2,36864]{2,1,0:T(2,128)(2,1)}), bf16[4,2,36864]{2,1,0:T(2,128)(2,1)}, u32[]{:S(2)}, u32[]{:S(2)}) async-start(bf16[4,2,36864]{2,1,0:T(2,128)(2,1)} %reshape.78), calls=%async_computation | async-start | bytes 1179648 | tf_op jit(solution)/shard_map/all_to_all | solution.py:61
  20.9 0.0 reduce-scatter.2.cloned.1.call-start
  20.9 0.0 copy-done.2
  20.9 0.6 dynamic_slice.13
  21.5 0.7 iota_compare_fusion.1
  22.2 0.1 select_reduce_fusion
  22.3 8.8 %all-to-all-done = bf16[4,2,36864]{2,1,0:T(2,128)(2,1)} async-done(((bf16[4,2,36864]{2,1,0:T(2,128)(2,1)}), bf16[4,2,36864]{2,1,0:T(2,128)(2,1)}, u32[]{:S(2)}, u32[]{:S(2)}) %all-to-all-start) | async-done | bytes 589856 | tf_op jit(solution)/shard_map/all_to_all | solution.py:61
  31.1 3.4 %reshape.79 = bf16[3072,3,32]{2,1,0:T(4,128)(2,1)S(1)} reshape(bf16[4,2,36864]{2,1,0:T(2,128)(2,1)} %all-to-all-done) | data formatting | bytes 1179648
  34.5 3.0 %copy.56 = bf16[4,32,3,768]{3,1,0,2:T(8,128)(2,1)} copy(bf16[4,32,3,768]{1,2,3,0:T(4,128)(2,1)S(1)} %bitcast.68) | data formatting | bytes 1179648 | tf_op jit(solution)/shard_map/all_to_all | solution.py:61
  37.5 1.2 %fusion.31 = (bf16[128,1,768]{2,0,1:T(8,128)(2,1)S(1)}, bf16[128,1,768]{2,0,1:T(8,128)(2,1)S(1)}, bf16[128,1,768]{2,0,1:T(8,128)(2,1)S(1)}) fusion(bf16[128,3,768]{2,0,1:T(8,128)(2,1)} %bitcast.70), kind=kLoop, calls=%fused_computation.52 | loop fusion | bytes 1179648 | tf_op jit(solution)/shard_map/slice | solution.py:64
  38.7 0.2 copy.57
  38.8 0.2 copy.58
  39.0 0.2 copy.61
  39.2 0.3 fusion.32
  39.5 11.1 %all-gather.2.cloned.1.call-done = bf16[512,2,768]{0,2,1:T(8,128)(2,1)} async-done(((bf16[128,2,768]{0,2,1:T(8,128)(2,1)}), bf16[512,2,768]{0,2,1:T(8,128)(2,1)}) %all-gather.2.cloned.1.call-update) | async-done | bytes 1572880 | tf_op jit(solution)/shard_map/all_gather | solution.py:78
  50.6 1.6 %fusion.33 = (f32[6,128]{1,0:T(8,128)S(1)}, f32[6,128,512]{2,1,0:T(8,128)S(1)}) fusion(bf16[128,6,128]{0,2,1:T(8,128)(2,1)S(1)} %bitcast.73, bf16[512,2,6,128]{0,3,2,1:T(8,128)(2,1)} %bitcast.76, pred[512]{0:T(512)(128)(4,1)S(1)} %fusion.26), kind=kOutput, calls=%fused_computation.54 | convolution fusion | flops 101842176 | bytes 2559488 | tf_op jit(solution)/shard_map/while/body/eval_jaxpr/qhe,khe->hqk/dot_general | solution.py:17
  52.2 0.0 copy-start.1
  52.2 0.1 fusion.12
  52.3 0.5 fusion
  52.8 0.3 fusion.6
  53.1 0.5 copy-done.1
  53.6 0.5 fusion.7
  54.1 0.0 copy-start
  54.1 4.1 %convolution_convert_fusion = bf16[128,3072]{1,0:T(8,128)(2,1)} fusion(bf16[128,768]{0,1:T(8,128)(2,1)S(1)} %bitcast.78, bf16[768,3072]{1,0:T(8,128)(2,1)} %param.8), kind=kOutput, calls=%fused_computation | convolution fusion | flops 604372992 | bytes 5701632 | tf_op jit(solution)/shard_map/dot_general | solution.py:90
  58.2 0.0 reduce-scatter.2.cloned.1.call-update
  58.9 0.8 dynamic-slice_convert_fusion
  59.7 0.0 copy-done
  59.7 1.2 %copy.66 = bf16[128,2,768]{2,1,0:T(2,128)(2,1)} copy(bf16[128,2,768]{2,0,1:T(8,128)(2,1)S(1)} %slice.31) | data formatting | bytes 786432
  60.9 19.0 %reduce-scatter.2.cloned.1.call-done = bf16[32,3072]{1,0:T(8,128)(2,1)} async-done(((bf16[128,3072]{1,0:T(8,128)(2,1)}), bf16[32,3072]{1,0:T(8,128)(2,1)}) %reduce-scatter.2.cloned.1.call-update) | async-done | bytes 196624 | tf_op jit(solution)/shard_map/reduce_scatter | solution.py:89
  79.9 1.6 %multiply_convert_fusion = bf16[32,3072]{1,0:T(8,128)(2,1)} fusion(bf16[32,3072]{1,0:T(8,128)(2,1)} %reduce-scatter.2.cloned.1.call-done, f32[3072]{0:T(1024)S(1)} %bitcast.79), kind=kLoop, calls=%fused_computation.19 | loop fusion | flops 294912 | bytes 405504 | tf_op jit(solution)/shard_map/convert_element_type | solution.py:96
  (5 shorter events, 0.1 us)
Async XLA Ops:
  7.2 43.4 %all-gather.2.cloned.1.call-start = ((), (), s32[]{:S(2)}) async-start(), calls=%async_computation.2 | async-start | bytes 1966080 | tf_op jit(solution)/shard_map/all_gather | solution.py:78
  13.6 7.3 %copy-start.2 = (s32[4]{0:T(128)S(1)}, s32[4]{0:T(128)}, u32[]{:S(2)}) copy-start(s32[4]{0:T(128)} %param.10) | copy-start | bytes 52
  16.7 14.4 %all-to-all-start = ((bf16[4,2,36864]{2,1,0:T(2,128)(2,1)}), bf16[4,2,36864]{2,1,0:T(2,128)(2,1)}, u32[]{:S(2)}, u32[]{:S(2)}) async-start(bf16[4,2,36864]{2,1,0:T(2,128)(2,1)} %reshape.78), calls=%async_computation | async-start | bytes 1179648 | tf_op jit(solution)/shard_map/all_to_all | solution.py:61
  20.9 59.0 %reduce-scatter.2.cloned.1.call-start = ((), (), s32[]{:S(2)}) async-start(), calls=%async_computation.3 | async-start | bytes 983040 | tf_op jit(solution)/shard_map/reduce_scatter | solution.py:89
  52.2 1.4 %copy-start.1 = (bf16[512,2,768]{0,2,1:T(8,128)(2,1)S(1)}, bf16[512,2,768]{0,2,1:T(8,128)(2,1)}, u32[]{:S(2)}) copy-start(bf16[512,2,768]{0,2,1:T(8,128)(2,1)} %all-gather.2.cloned.1.call-done) | copy-start | bytes 4718596
  54.1 5.6 %copy-start = (bf16[4,32,3,768]{3,1,0,2:T(8,128)(2,1)S(1)}, bf16[4,32,3,768]{3,1,0,2:T(8,128)(2,1)}, u32[]{:S(2)}) copy-start(bf16[4,32,3,768]{3,1,0,2:T(8,128)(2,1)} %copy.56) | copy-start | bytes 1769476
Sparse Core Ops, SparseCore 0:
  10.1 40.3 all-gather.1
  58.3 21.4 reduce-scatter.1
where the time goes:
time: 88.9 us; the launch traced here: 88.3 us
  waiting for transfers between devices  38.9 us (44%)
  local copies, waits for them, and re-layouts  19.8 us (22%)
  between operations  14.8 us (17%)
  matrix products  6.74 us (8%)
  starting transfers between devices  4.25 us (5%)
  other arithmetic  3.8 us (4%)
    reduce_scatter x1, waiting for transfers between devices, shards(): lax.psum_scatter(jnp.dot(attended, w_out, preferred_element_type=jnp.floa...  19 us
    unnamed x11, local copies, waits for them, and re-layouts  14.6 us
    all_gather x1, waiting for transfers between devices, shards(): gathered = lax.all_gather(stale_kv, 'patch', axis=0, tiled=True)  11.1 us
    all_to_all x1, waiting for transfers between devices, shards(): lax.all_to_all(qkv, 'head', split_axis=2, concat_axis=0, tiled=True)  8.81 us
    all_to_all x1, starting transfers between devices, shards(): lax.all_to_all(qkv, 'head', split_axis=2, concat_axis=0, tiled=True)  4.21 us
    dot_general x1, matrix products, shards(): jnp.dot(attended, w_out, preferred_element_type=jnp.float32)  4.1 us
    all_to_all x1, local copies, waits for them, and re-layouts, shards(): lax.all_to_all(qkv, 'head', split_axis=2, concat_axis=0, tiled=True)  2.98 us
    dot_general x2, matrix products, attend_block(): jnp.einsum('qhe,khe->hqk', queries, keys_here, preferred_element_type=jnp...  1.91 us
  transfers between devices with their start and end apart: 3, of which 3 were waited for; matrix products, arithmetic and copies ran while one was open for 22% of the time, Pallas kernels for 0%

commit v1 on v0

v1 whole, which is shorter than its diff:
```python
import math

import jax
import jax.numpy as jnp
from jax import lax
from jax.experimental import pallas as pl
from jax.experimental.pallas import tpu as pltpu
from jax.sharding import PartitionSpec as P

HEAD_DIM = 128
MASKED = -1e30
VMEM = pl.BlockSpec(memory_space=pltpu.VMEM)
SMEM = pl.BlockSpec(memory_space=pltpu.SMEM)
ANY = pl.BlockSpec(memory_space=pl.ANY)


def params():
    return pltpu.CompilerParams(vmem_limit_bytes=48 * 1024 * 1024)


def ring_order(count):
    return list(range(0, count, 1)) if count < 3 else (
        [0] + list(range(1, count, 2)) + list(range((count - 1) // 2 * 2, 0, -2))
    )


def split_qkv(qkv_t, n_head):
    planes, rows, width = qkv_t.shape
    columns = width // n_head

    def kernel(src, *rest):
        outs, sems = rest[:n_head], rest[n_head]
        mine = lax.axis_index("head")
        copies = []
        for j in range(n_head):
            start = pl.multiple_of((mine ^ j) * columns, columns)
            copies.append(
                pltpu.make_async_copy(src.at[:, :, pl.ds(start, columns)], outs[j], sems.at[j])
            )
        for copy in copies:
            copy.start()
        for copy in copies:
            copy.wait()

    return pl.pallas_call(
        kernel,
        out_shape=[jax.ShapeDtypeStruct((planes, rows, columns), qkv_t.dtype)] * n_head,
        in_specs=[ANY],
        out_specs=[ANY] * n_head,
        scratch_shapes=[pltpu.SemaphoreType.DMA((n_head,))],
        compiler_params=params(),
    )(qkv_t)


def padded(rows):
    return -(-rows // 128) * 128


def weigh(lengths, pieces, stale_keys, origins):
    n_head = len(pieces)
    _, tok_rows, columns = pieces[0].shape
    rows = n_head * tok_rows
    heads = columns // HEAD_DIM
    keep = max(1, rows * 3 // 4)
    per_array = [array.shape[0] // keep for array in stale_keys]
    blocks = sum(per_array)
    pitch = padded(keep)
    total = padded(rows) + blocks * pitch
    scale = 1.0 / math.sqrt(HEAD_DIM)

    def kernel(lengths_ref, *rest):
        piece_refs = rest[:n_head]
        key_refs = rest[n_head : n_head + len(stale_keys)]
        weights_ref, sums_ref, kv_ref, query_buf, key_buf = rest[n_head + len(stale_keys) :]
        mine = lax.axis_index("head")
        patch = lax.axis_index("patch")
        own_limit = lengths_ref[patch]
        position = lax.broadcasted_iota(jnp.int32, (1, tok_rows), 1)
        live_parts = []
        for j in range(n_head):
            here = pl.ds(j * tok_rows, tok_rows)
            query_buf[here, :] = piece_refs[j][0]
            key_buf[here, :] = piece_refs[j][1]
            there = pl.ds(pl.multiple_of((mine ^ j) * tok_rows, tok_rows), tok_rows)
            kv_ref[0, there, :] = piece_refs[j][1]
            kv_ref[1, there, :] = piece_refs[j][2]
        column = lax.broadcasted_iota(jnp.int32, (1, rows), 1)
        absolute = ((column // tok_rows) ^ mine) * tok_rows + column % tok_rows
        fresh_live = absolute < own_limit
        stale_row = lax.broadcasted_iota(jnp.int32, (1, keep), 1)
        limits = origins(lengths_ref, patch)
        for head in range(heads):
            lanes = slice(head * HEAD_DIM, (head + 1) * HEAD_DIM)
            queries = query_buf[:, lanes]

            def score(keys, live):
                found = lax.dot_general(
                    queries, keys, (((1,), (1,)), ((), ())), preferred_element_type=jnp.float32
                )
                return jnp.where(live, found * scale, MASKED)

            parts = [score(key_buf[:, lanes], fresh_live)]
            number = 0
            for ref, count in zip(key_refs, per_array):
                for block in range(count):
                    keys = ref[block * keep : (block + 1) * keep, lanes]
                    parts.append(score(keys, stale_row < limits[number]))
                    number += 1
            top = jnp.max(parts[0], axis=1, keepdims=True)
            for part in parts[1:]:
                top = jnp.maximum(top, jnp.max(part, axis=1, keepdims=True))
            weight_sum = jnp.zeros_like(top)
            for number, part in enumerate(parts):
                weights = jnp.exp(part - top)
                weight_sum = weight_sum + jnp.sum(weights, axis=1, keepdims=True)
                first = 0 if number == 0 else padded(rows) + (number - 1) * pitch
                weights_ref[head, :, first : first + part.shape[1]] = weights.astype(jnp.bfloat16)
            sums_ref[head] = weight_sum

    return pl.pallas_call(
        kernel,
        out_shape=[
            jax.ShapeDtypeStruct((heads, rows, total), jnp.bfloat16),
            jax.ShapeDtypeStruct((heads, rows, 1), jnp.float32),
            jax.ShapeDtypeStruct((2, rows, columns), jnp.bfloat16),
        ],
        in_specs=[SMEM] + [VMEM] * (n_head + len(stale_keys)),
        out_specs=[VMEM] * 3,
        scratch_shapes=[
            pltpu.VMEM((rows, columns), jnp.bfloat16),
            pltpu.VMEM((rows, columns), jnp.bfloat16),
        ],
        compiler_params=params(),
    )(lengths, *pieces, *stale_keys)


def project(weights, sums, pieces, stale_values, w_out, which):
    n_head = len(pieces)
    _, tok_rows, columns = pieces[0].shape
    rows = n_head * tok_rows
    heads = columns // HEAD_DIM
    keep = max(1, rows * 3 // 4)
    per_array = [array.shape[0] // keep for array in stale_values]
    pitch = padded(keep)
    model = w_out.shape[1]
    first_row, row_count = which[0] * tok_rows, len(which) * tok_rows

    def kernel(weights_ref, sums_ref, *rest):
        piece_refs = rest[:n_head]
        value_refs = rest[n_head : n_head + len(stale_values)]
        w_ref = rest[n_head + len(stale_values)]
        out_refs = rest[n_head + len(stale_values) + 1 : -2]
        value_buf, attended_buf = rest[-2:]
        here = slice(first_row, first_row + row_count)
        for j in range(n_head):
            value_buf[j * tok_rows : (j + 1) * tok_rows, :] = piece_refs[j][2]
        for head in range(heads):
            lanes = slice(head * HEAD_DIM, (head + 1) * HEAD_DIM)
            mixed = jnp.dot(
                weights_ref[head, here, :rows],
                value_buf[:, lanes],
                preferred_element_type=jnp.float32,
            )
            first = padded(rows)
            for ref, count in zip(value_refs, per_array):
                for block in range(count):
                    mixed = mixed + jnp.dot(
                        weights_ref[head, here, first : first + keep],
                        ref[block * keep : (block + 1) * keep, lanes],
                        preferred_element_type=jnp.float32,
                    )
                    first += pitch
            attended_buf[:, lanes] = (mixed / sums_ref[head, here, :]).astype(jnp.bfloat16)
        result = jnp.dot(attended_buf[...], w_ref[...], preferred_element_type=jnp.float32)
        for number, ref in enumerate(out_refs):
            ref[...] = result[number * tok_rows : (number + 1) * tok_rows].astype(ref.dtype)

    return pl.pallas_call(
        kernel,
        out_shape=[jax.ShapeDtypeStruct((tok_rows, model), jnp.bfloat16)] * len(which),
        in_specs=[VMEM] * (3 + n_head + len(stale_values)),
        out_specs=[VMEM] * len(which),
        scratch_shapes=[
            pltpu.VMEM((rows, columns), jnp.bfloat16),
            pltpu.VMEM((row_count, columns), jnp.bfloat16),
        ],
        compiler_params=params(),
    )(weights, sums, *pieces, *stale_values, w_out)


def add_pair(left, right):
    return (left.astype(jnp.float32) + right.astype(jnp.float32)).astype(jnp.bfloat16)


def build(n_head, n_patch):
    flip = [[(i, i ^ j) for i in range(n_head)] for j in range(n_head)]
    order = ring_order(n_patch)
    ring = [(order[i], order[(i + 1) % n_patch]) for i in range(n_patch)]
    on_line = n_patch <= 4

    def ring_limits(lengths_ref, patch):
        place = sum(jnp.where(patch == order[i], i, 0) for i in range(n_patch))
        limits = []
        for step in range(1, n_patch):
            back = lax.rem(place + n_patch - step, n_patch)
            origin = sum(jnp.where(back == i, order[i], 0) for i in range(n_patch))
            limits.append(lengths_ref[origin])
        return limits

    def gathered_limits(lengths_ref, patch):
        return [jnp.where(patch == i, 0, lengths_ref[i]) for i in range(n_patch)]

    def shards(qkv, stale_kv, w_out, gate_table, lengths, timestep):
        patch_rows = stale_kv.shape[0]
        keep = patch_rows * 3 // 4
        stale_k, stale_v = stale_kv[:keep, 0], stale_kv[:keep, 1]
        if on_line:
            keys, values = [stale_k], [stale_v]
            for _ in range(n_patch - 1):
                keys.append(lax.ppermute(keys[-1], "patch", ring))
                values.append(lax.ppermute(values[-1], "patch", ring))
            keys, values, origins = keys[1:], values[1:], ring_limits
        else:
            keys = [lax.all_gather(stale_k, "patch", axis=0, tiled=True)]
            values = [lax.all_gather(stale_v, "patch", axis=0, tiled=True)]
            origins = gathered_limits
        sent = split_qkv(jnp.transpose(qkv, (1, 0, 2)), n_head)
        pieces = [sent[0]] + [lax.ppermute(sent[j], "head", flip[j]) for j in range(1, n_head)]
        weights, sums, next_t = weigh(lengths, pieces, keys, origins)
        next_kv = jnp.transpose(next_t, (1, 0, 2))

        half = n_head // 2
        far = project(weights, sums, pieces, values, w_out, range(half, n_head))
        near = project(weights, sums, pieces, values, w_out, range(0, half))
        held = list(near) + list(far)
        bit = 1
        while bit < n_head:
            merged = [None] * n_head
            for j in reversed(range(n_head)):
                if j % (2 * bit) == 0:
                    arrived = lax.ppermute(held[j + bit], "head", flip[bit])
                    if 2 * bit < n_head:
                        merged[j] = add_pair(held[j], arrived)
                    else:
                        merged[j] = held[j].astype(jnp.float32) + arrived.astype(jnp.float32)
            held = merged
            bit *= 2
        projected = held[0].astype(jnp.float32)
        gate_row = lax.dynamic_slice_in_dim(gate_table, timestep[0], 1, 0)[0].astype(jnp.float32)
        branch = (gate_row[None, :] * projected).astype(jnp.bfloat16)
        return (branch, next_kv)

    return shards


def solution(mesh):
    return jax.shard_map(
        build(mesh.shape["head"], mesh.shape["patch"]),
        mesh=mesh,
        in_specs=(
            P(("groups", "patch", "head"), None, None),
            P(("groups", "patch"), None, "head"),
            P("head", None),
            P(),
            P("groups"),
            P("groups"),
        ),
        out_specs=(P(("groups", "patch", "head"), None), P(("groups", "patch"), None, "head")),
        check_vma=False,
    )
```

time: 88.9 us -> 45.3 us (0.51)
  waiting for transfers between devices: 38.9 us -> 10.9 us
  local copies, waits for them, and re-layouts: 19.8 us -> 4.47 us
  between operations: 14.8 us -> 1.37 us
  starting transfers between devices: 4.25 us -> 17.5 us
  Pallas kernels: 0 us -> 9.07 us
  matrix products: 6.74 us -> 0 us
  other arithmetic: 3.8 us -> 1.62 us
    reduce_scatter x1 -> x0, waiting for transfers between devices: 19 us -> none  [shards(): lax.psum_scatter(jnp.dot(attended, w_out, preferred_element_type=jnp.floa...]
    ppermute x0 -> x12, starting transfers between devices: none -> 17.5 us  [the longest x3 6.88 us: shards(): keys.append(lax.ppermute(keys[-1], 'patch', ring))]
    unnamed x11 -> x7, local copies, waits for them, and re-layouts: 14.6 us -> 2.91 us
    all_gather x1 -> x0, waiting for transfers between devices: 11.1 us -> none  [shards(): gathered = lax.all_gather(stale_kv, 'patch', axis=0, tiled=True)]
    ppermute x0 -> x12, waiting for transfers between devices: none -> 10.9 us  [the longest x3 3.49 us: shards(): keys.append(lax.ppermute(keys[-1], 'patch', ring))]
    pallas_call x0 -> x4, Pallas kernels: none -> 9.07 us  [the longest x2 6.99 us: project(): pl.pallas_call(kernel, out_shape=[jax.ShapeDtypeStruct((tok_rows, model),...]
    all_to_all x1 -> x0, waiting for transfers between devices: 8.81 us -> none  [shards(): lax.all_to_all(qkv, 'head', split_axis=2, concat_axis=0, tiled=True)]
    dot_general x5 -> x0, matrix products: 6.74 us -> none  [the longest x1 4.1 us: shards(): jnp.dot(attended, w_out, preferred_element_type=jnp.float32)]
  transfers between devices with their start and end apart: 3 -> 12, of which waited for: 3 -> 6; matrix products, arithmetic and copies ran while one was open for 22% -> 5% of each run, Pallas kernels for 0% -> 12%
where the time goes in v1:
time: 45.3 us; the launch traced here: 45 us
  starting transfers between devices  17.5 us (39%)
  waiting for transfers between devices  10.9 us (24%)
  Pallas kernels  9.07 us (20%)
  local copies, waits for them, and re-layouts  4.47 us (10%)
  other arithmetic  1.62 us (4%)
  between operations  1.37 us (3%)
    pallas_call x2, Pallas kernels, project(): pl.pallas_call(kernel, out_shape=[jax.ShapeDtypeStruct((tok_rows, model),...  6.99 us
    ppermute x3, starting transfers between devices, shards(): keys.append(lax.ppermute(keys[-1], 'patch', ring))  6.88 us
    ppermute x3, starting transfers between devices, shards(): values.append(lax.ppermute(values[-1], 'patch', ring))  6.35 us
    ppermute x3, waiting for transfers between devices, shards(): keys.append(lax.ppermute(keys[-1], 'patch', ring))  3.49 us
    ppermute x3, waiting for transfers between devices, shards(): arrived = lax.ppermute(held[j + bit], 'head', flip[bit])  3.31 us
    unnamed x7, local copies, waits for them, and re-layouts  2.91 us
    ppermute x3, waiting for transfers between devices, shards(): lax.ppermute(sent[j], 'head', flip[j])  2.63 us
    ppermute x3, starting transfers between devices, shards(): arrived = lax.ppermute(held[j + bit], 'head', flip[bit])  2.35 us
  transfers between devices with their start and end apart: 12, of which 6 were waited for; matrix products, arithmetic and copies ran while one was open for 5% of the time, Pallas kernels for 12%

profile of v1, /device:TPU:0, one launch (start us, length us, event | category | flops | bytes accessed | tf_op | source)
XLA Modules:
  0.0 45.0 jit_solution(7172026729168586173)
XLA Ops:
  0.6 1.6 %fusion = (bf16[96,1,768]{2,1,0:T(2,128)(2,1)S(1)}, bf16[96,1,768]{2,1,0:T(2,128)(2,1)S(1)}) fusion(bf16[128,2,768]{2,1,0:T(2,128)(2,1)} %param.7), kind=kLoop, calls=%fused_computation.6 | loop fusion | bytes 589824 | tf_op jit(solution)/shard_map/slice | solution.py:216
  2.2 3.1 %collective-permute-start.3 = (bf16[96,768]{1,0:T(8,128)(2,1)S(1)}, bf16[96,768]{1,0:T(8,128)(2,1)S(1)}, u32[]{:S(2)}, u32[]{:S(2)}) collective-permute-start(bf16[96,768]{1,0:T(8,128)(2,1)S(1)} %bitcast.16), channel_id=1, source_target_pairs={{0,4},{4,12},{12,8},{8,0},{1,5},{5,13},{13,9},{9,1},{2,6},{6,14},{... | collective-permute-start | bytes 442376 | tf_op jit(solution)/shard_map/ppermute | solution.py:220
  5.3 2.6 %collective-permute-start.6 = (bf16[96,768]{1,0:T(8,128)(2,1)S(1)}, bf16[96,768]{1,0:T(8,128)(2,1)S(1)}, u32[]{:S(2)}, u32[]{:S(2)}) collective-permute-start(bf16[96,768]{1,0:T(8,128)(2,1)S(1)} %bitcast.15), channel_id=1, source_target_pairs={{0,4},{4,12},{12,8},{8,0},{1,5},{5,13},{13,9},{9,1},{2,6},{6,14},{... | collective-permute-start | bytes 442376 | tf_op jit(solution)/shard_map/ppermute | solution.py:221
  8.0 3.0 %collective-permute-done.3.rest_4_ = bf16[96,768]{1,0:T(8,128)(2,1)S(1)} collective-permute-done((bf16[96,768]{1,0:T(8,128)(2,1)S(1)}, bf16[96,768]{1,0:T(8,128)(2,1)S(1)}, u32[]{:S(2)}, u32[]{:S(2)}) %collective-permute-start.3) | collective-permute-done | bytes 147488 | tf_op jit(solution)/shard_map/ppermute | solution.py:220
  11.0 1.2 %collective-permute-start.4 = (bf16[96,768]{1,0:T(8,128)(2,1)S(1)}, bf16[96,768]{1,0:T(8,128)(2,1)S(1)}, u32[]{:S(2)}, u32[]{:S(2)}) collective-permute-start(bf16[96,768]{1,0:T(8,128)(2,1)S(1)} %collective-permute-done.3.rest_4_), channel_id=1, source_target_pairs={{0,4},{4,12},{12,8},{8,0},{1,5},{5,13},{13,9},{9,1},{2,6},{6,14},{... | collective-permute-start | bytes 442376 | tf_op jit(solution)/shard_map/ppermute | solution.py:220
  12.1 1.5 %collective-permute-done.6.rest_4_ = bf16[96,768]{1,0:T(8,128)(2,1)S(1)} collective-permute-done((bf16[96,768]{1,0:T(8,128)(2,1)S(1)}, bf16[96,768]{1,0:T(8,128)(2,1)S(1)}, u32[]{:S(2)}, u32[]{:S(2)}) %collective-permute-start.6) | collective-permute-done | bytes 147488 | tf_op jit(solution)/shard_map/ppermute | solution.py:221
  13.6 1.9 %collective-permute-start.7 = (bf16[96,768]{1,0:T(8,128)(2,1)S(1)}, bf16[96,768]{1,0:T(8,128)(2,1)S(1)}, u32[]{:S(2)}, u32[]{:S(2)}) collective-permute-start(bf16[96,768]{1,0:T(8,128)(2,1)S(1)} %collective-permute-done.6.rest_4_), channel_id=1, source_target_pairs={{0,4},{4,12},{12,8},{8,0},{1,5},{5,13},{13,9},{9,1},{2,6},{6,14},{... | collective-permute-start | bytes 442376 | tf_op jit(solution)/shard_map/ppermute | solution.py:221
  15.5 0.0 copy-start
  15.5 1.1 %copy-done = bf16[32,3,3072]{2,0,1:T(8,128)(2,1)S(1)} copy-done((bf16[32,3,3072]{2,0,1:T(8,128)(2,1)S(1)}, bf16[32,3,3072]{2,0,1:T(8,128)(2,1)}, u32[]{:S(2)}) %copy-start) | copy-done | bytes 589848
  16.6 0.1 shard_map.77
  16.7 0.1 collective-permute-start
  16.8 1.6 %collective-permute-start.1 = (bf16[3,32,768]{2,1,0:T(8,128)(2,1)S(1)}, bf16[3,32,768]{2,1,0:T(8,128)(2,1)S(1)}, u32[]{:S(2)}, u32[]{:S(2)}) collective-permute-start(bf16[3,32,768]{2,1,0:T(8,128)(2,1)S(1)} %get-tuple-element.15), channel_id=1, source_target_pairs={{0,2},{1,3},{2,0},{3,1},{4,6},{5,7},{6,4},{7,5},{8,10},{9,11},{10,... | collective-permute-start | bytes 442376 | tf_op jit(solution)/shard_map/ppermute | solution.py:228
  18.4 0.3 collective-permute-start.2
  18.7 0.0 collective-permute-done.4.rest_5_
  18.7 2.6 %collective-permute-start.5 = (bf16[96,768]{1,0:T(8,128)(2,1)S(1)}, bf16[96,768]{1,0:T(8,128)(2,1)S(1)}, u32[]{:S(2)}, u32[]{:S(2)}) collective-permute-start(bf16[96,768]{1,0:T(8,128)(2,1)S(1)} %collective-permute-done.4.rest_5_), channel_id=1, source_target_pairs={{0,4},{4,12},{12,8},{8,0},{1,5},{5,13},{13,9},{9,1},{2,6},{6,14},{... | collective-permute-start | bytes 442376 | tf_op jit(solution)/shard_map/ppermute | solution.py:220
  21.3 0.0 collective-permute-done.7.rest_5_
  21.3 1.8 %collective-permute-start.8 = (bf16[96,768]{1,0:T(8,128)(2,1)S(1)}, bf16[96,768]{1,0:T(8,128)(2,1)S(1)}, u32[]{:S(2)}, u32[]{:S(2)}) collective-permute-start(bf16[96,768]{1,0:T(8,128)(2,1)S(1)} %collective-permute-done.7.rest_5_), channel_id=1, source_target_pairs={{0,4},{4,12},{12,8},{8,0},{1,5},{5,13},{13,9},{9,1},{2,6},{6,14},{... | collective-permute-start | bytes 442376 | tf_op jit(solution)/shard_map/ppermute | solution.py:221
  23.1 0.0 collective-permute-done.rest_1_
  23.1 0.4 collective-permute-done.1.rest_2_
  23.5 2.3 %collective-permute-done.2.rest_3_ = bf16[3,32,768]{2,1,0:T(8,128)(2,1)S(1)} collective-permute-done((bf16[3,32,768]{2,1,0:T(8,128)(2,1)S(1)}, bf16[3,32,768]{2,1,0:T(8,128)(2,1)S(1)}, u32[]{:S(2)}, u32[]{:S(2)}) %collective-permute-start.2) | collective-permute-done | bytes 147488 | tf_op jit(solution)/shard_map/ppermute | solution.py:228
  25.8 0.5 %collective-permute-done.5.rest_6_ = bf16[96,768]{1,0:T(8,128)(2,1)S(1)} collective-permute-done((bf16[96,768]{1,0:T(8,128)(2,1)S(1)}, bf16[96,768]{1,0:T(8,128)(2,1)S(1)}, u32[]{:S(2)}, u32[]{:S(2)}) %collective-permute-start.5) | collective-permute-done | bytes 147488 | tf_op jit(solution)/shard_map/ppermute | solution.py:220
  26.2 0.0 copy-start.1
  26.2 0.7 %copy-done.1 = s32[4]{0:T(128)S(1)} copy-done((s32[4]{0:T(128)S(1)}, s32[4]{0:T(128)}, u32[]{:S(2)}) %copy-start.1) | copy-done | bytes 40
  26.9 2.0 %shard_map.78 = (bf16[6,128,512]{2,1,0:T(8,128)(2,1)S(1)}, f32[6,128,1]{2,1,0:T(8,128)S(1)}, bf16[2,128,768]{2,1,0:T(8,128)(2,1)S(1)}) custom-call(s32[4]{0:T(128)S(1)} %copy-done.1, bf16[3,32,768]{2,1,0:T(8,128)(2,1)S(1)} %get-tuple-element.13.rest_0_, bf16[3,32,768]{2,1,0:T(8,128)(2,1)S(1)} %collective-permute-done.rest_1_, ...), custom_call_target="tpu_custom_call" | custom-call | tf_op jit(solution)/shard_map/pallas_call | solution.py:120
  28.8 0.0 collective-permute-done.8.rest_6_
  28.9 3.5 %shard_map.80 = (bf16[32,3072]{1,0:T(8,128)(2,1)S(1)}, bf16[32,3072]{1,0:T(8,128)(2,1)S(1)}) custom-call(bf16[6,128,512]{2,1,0:T(8,128)(2,1)S(1)} %get-tuple-element.17.weights_ref, f32[6,128,1]{2,1,0:T(8,128)S(1)} %get-tuple-element.18.sums_ref, bf16[3,32,768]{2,1,0:T(8,128)(2,1)S(1)} %get-tuple-element.13.rest_0_, ...), custom_call_target="tpu_custom_call" | custom-call | tf_op jit(solution)/shard_map/pallas_call | solution.py:178
  32.4 0.2 collective-permute-start.10
  33.2 3.5 %shard_map.79 = (bf16[32,3072]{1,0:T(8,128)(2,1)S(1)}, bf16[32,3072]{1,0:T(8,128)(2,1)S(1)}) custom-call(bf16[6,128,512]{2,1,0:T(8,128)(2,1)S(1)} %get-tuple-element.17.weights_ref, f32[6,128,1]{2,1,0:T(8,128)S(1)} %get-tuple-element.18.sums_ref, bf16[3,32,768]{2,1,0:T(8,128)(2,1)S(1)} %get-tuple-element.13.rest_0_, ...), custom_call_target="tpu_custom_call" | custom-call | tf_op jit(solution)/shard_map/pallas_call | solution.py:178
  36.7 0.5 %collective-permute-start.9 = (bf16[32,3072]{1,0:T(8,128)(2,1)S(1)}, bf16[32,3072]{1,0:T(8,128)(2,1)S(1)}, u32[]{:S(2)}, u32[]{:S(2)}) collective-permute-start(bf16[32,3072]{1,0:T(8,128)(2,1)S(1)} %get-tuple-element.20), channel_id=1, source_target_pairs={{0,1},{1,0},{2,3},{3,2},{4,5},{5,4},{6,7},{7,6},{8,9},{9,8},{10,11... | collective-permute-start | bytes 589832 | tf_op jit(solution)/shard_map/ppermute | solution.py:241
  37.2 0.0 collective-permute-done.10
  37.2 1.7 %collective-permute-start.11 = (bf16[32,3072]{1,0:T(8,128)(2,1)S(1)}, bf16[32,3072]{1,0:T(8,128)(2,1)S(1)}, u32[]{:S(2)}, u32[]{:S(2)}) collective-permute-start(bf16[32,3072]{1,0:T(8,128)(2,1)S(1)} %add_convert_fusion), channel_id=1, source_target_pairs={{0,2},{1,3},{2,0},{3,1},{4,6},{5,7},{6,4},{7,5},{8,10},{9,11},{10,... | collective-permute-start | bytes 589832 | tf_op jit(solution)/shard_map/ppermute | solution.py:241
  38.9 0.8 %dynamic-slice_convert_fusion = f32[1,3072]{1,0:T(1,128)S(1)} fusion(bf16[50,3072]{1,0:T(8,128)(2,1)} %param.9, s32[]{:T(128)S(6)} %select_n.3), kind=kLoop, calls=%fused_computation.5 | loop fusion | flops 3072 | bytes 18436 | tf_op jit(solution)/shard_map/mul | solution.py:250
  39.7 1.2 %copy.10 = bf16[128,2,768]{2,1,0:T(2,128)(2,1)} copy(bf16[128,2,768]{2,0,1:T(8,128)(2,1)S(1)} %bitcast.14) | data formatting | bytes 786432
  40.9 0.0 collective-permute-done.9
  40.9 3.3 %collective-permute-done.11 = bf16[32,3072]{1,0:T(8,128)(2,1)S(1)} collective-permute-done((bf16[32,3072]{1,0:T(8,128)(2,1)S(1)}, bf16[32,3072]{1,0:T(8,128)(2,1)S(1)}, u32[]{:S(2)}, u32[]{:S(2)}) %collective-permute-start.11) | collective-permute-done | bytes 196640 | tf_op jit(solution)/shard_map/ppermute | solution.py:241
  44.2 0.8 %multiply_convert_fusion = bf16[32,3072]{1,0:T(8,128)(2,1)} fusion(bf16[32,3072]{1,0:T(8,128)(2,1)S(1)} %collective-permute-done.11, bf16[32,3072]{1,0:T(8,128)(2,1)S(1)} %collective-permute-done.9, bf16[32,3072]{1,0:T(8,128)(2,1)S(1)} %get-tuple-element.19, f32[3072]{0:T(1024)S(1)} %bitcast.17), kind=kLoop, calls=%fused_computation | loop fusion | flops 884736 | bytes 798720 | tf_op jit(solution)/shard_map/convert_element_type | solution.py:250
  (3 shorter events, 0.1 us)
Async XLA Ops:
  2.2 8.8 %collective-permute-start.3 = (bf16[96,768]{1,0:T(8,128)(2,1)S(1)}, bf16[96,768]{1,0:T(8,128)(2,1)S(1)}, u32[]{:S(2)}, u32[]{:S(2)}) collective-permute-start(bf16[96,768]{1,0:T(8,128)(2,1)S(1)} %bitcast.16), channel_id=1, source_target_pairs={{0,4},{4,12},{12,8},{8,0},{1,5},{5,13},{13,9},{9,1},{2,6},{6,14},{... | collective-permute-start | bytes 442376 | tf_op jit(solution)/shard_map/ppermute | solution.py:220
  5.3 8.3 %collective-permute-start.6 = (bf16[96,768]{1,0:T(8,128)(2,1)S(1)}, bf16[96,768]{1,0:T(8,128)(2,1)S(1)}, u32[]{:S(2)}, u32[]{:S(2)}) collective-permute-start(bf16[96,768]{1,0:T(8,128)(2,1)S(1)} %bitcast.15), channel_id=1, source_target_pairs={{0,4},{4,12},{12,8},{8,0},{1,5},{5,13},{13,9},{9,1},{2,6},{6,14},{... | collective-permute-start | bytes 442376 | tf_op jit(solution)/shard_map/ppermute | solution.py:221
  11.0 7.7 %collective-permute-start.4 = (bf16[96,768]{1,0:T(8,128)(2,1)S(1)}, bf16[96,768]{1,0:T(8,128)(2,1)S(1)}, u32[]{:S(2)}, u32[]{:S(2)}) collective-permute-start(bf16[96,768]{1,0:T(8,128)(2,1)S(1)} %collective-permute-done.3.rest_4_), channel_id=1, source_target_pairs={{0,4},{4,12},{12,8},{8,0},{1,5},{5,13},{13,9},{9,1},{2,6},{6,14},{... | collective-permute-start | bytes 442376 | tf_op jit(solution)/shard_map/ppermute | solution.py:220
  13.6 7.7 %collective-permute-start.7 = (bf16[96,768]{1,0:T(8,128)(2,1)S(1)}, bf16[96,768]{1,0:T(8,128)(2,1)S(1)}, u32[]{:S(2)}, u32[]{:S(2)}) collective-permute-start(bf16[96,768]{1,0:T(8,128)(2,1)S(1)} %collective-permute-done.6.rest_4_), channel_id=1, source_target_pairs={{0,4},{4,12},{12,8},{8,0},{1,5},{5,13},{13,9},{9,1},{2,6},{6,14},{... | collective-permute-start | bytes 442376 | tf_op jit(solution)/shard_map/ppermute | solution.py:221
  15.5 1.1 %copy-start = (bf16[32,3,3072]{2,0,1:T(8,128)(2,1)S(1)}, bf16[32,3,3072]{2,0,1:T(8,128)(2,1)}, u32[]{:S(2)}) copy-start(bf16[32,3,3072]{2,0,1:T(8,128)(2,1)} %param.6) | copy-start | bytes 1769476
  16.7 6.4 %collective-permute-start = (bf16[3,32,768]{2,1,0:T(8,128)(2,1)S(1)}, bf16[3,32,768]{2,1,0:T(8,128)(2,1)S(1)}, u32[]{:S(2)}, u32[]{:S(2)}) collective-permute-start(bf16[3,32,768]{2,1,0:T(8,128)(2,1)S(1)} %get-tuple-element.14), channel_id=1, source_target_pairs={{0,1},{1,0},{2,3},{3,2},{4,5},{5,4},{6,7},{7,6},{8,9},{9,8},{10,11... | collective-permute-start | bytes 442376 | tf_op jit(solution)/shard_map/ppermute | solution.py:228
  16.8 6.7 %collective-permute-start.1 = (bf16[3,32,768]{2,1,0:T(8,128)(2,1)S(1)}, bf16[3,32,768]{2,1,0:T(8,128)(2,1)S(1)}, u32[]{:S(2)}, u32[]{:S(2)}) collective-permute-start(bf16[3,32,768]{2,1,0:T(8,128)(2,1)S(1)} %get-tuple-element.15), channel_id=1, source_target_pairs={{0,2},{1,3},{2,0},{3,1},{4,6},{5,7},{6,4},{7,5},{8,10},{9,11},{10,... | collective-permute-start | bytes 442376 | tf_op jit(solution)/shard_map/ppermute | solution.py:228
  18.4 7.4 %collective-permute-start.2 = (bf16[3,32,768]{2,1,0:T(8,128)(2,1)S(1)}, bf16[3,32,768]{2,1,0:T(8,128)(2,1)S(1)}, u32[]{:S(2)}, u32[]{:S(2)}) collective-permute-start(bf16[3,32,768]{2,1,0:T(8,128)(2,1)S(1)} %get-tuple-element.16), channel_id=1, source_target_pairs={{0,3},{1,2},{2,1},{3,0},{4,7},{5,6},{6,5},{7,4},{8,11},{9,10},{10,... | collective-permute-start | bytes 442376 | tf_op jit(solution)/shard_map/ppermute | solution.py:228
  18.7 7.6 %collective-permute-start.5 = (bf16[96,768]{1,0:T(8,128)(2,1)S(1)}, bf16[96,768]{1,0:T(8,128)(2,1)S(1)}, u32[]{:S(2)}, u32[]{:S(2)}) collective-permute-start(bf16[96,768]{1,0:T(8,128)(2,1)S(1)} %collective-permute-done.4.rest_5_), channel_id=1, source_target_pairs={{0,4},{4,12},{12,8},{8,0},{1,5},{5,13},{13,9},{9,1},{2,6},{6,14},{... | collective-permute-start | bytes 442376 | tf_op jit(solution)/shard_map/ppermute | solution.py:220
  21.3 7.5 %collective-permute-start.8 = (bf16[96,768]{1,0:T(8,128)(2,1)S(1)}, bf16[96,768]{1,0:T(8,128)(2,1)S(1)}, u32[]{:S(2)}, u32[]{:S(2)}) collective-permute-start(bf16[96,768]{1,0:T(8,128)(2,1)S(1)} %collective-permute-done.7.rest_5_), channel_id=1, source_target_pairs={{0,4},{4,12},{12,8},{8,0},{1,5},{5,13},{13,9},{9,1},{2,6},{6,14},{... | collective-permute-start | bytes 442376 | tf_op jit(solution)/shard_map/ppermute | solution.py:221
  26.2 0.7 %copy-start.1 = (s32[4]{0:T(128)S(1)}, s32[4]{0:T(128)}, u32[]{:S(2)}) copy-start(s32[4]{0:T(128)} %lengths_ref.1) | copy-start | bytes 52
  32.4 4.8 %collective-permute-start.10 = (bf16[32,3072]{1,0:T(8,128)(2,1)S(1)}, bf16[32,3072]{1,0:T(8,128)(2,1)S(1)}, u32[]{:S(2)}, u32[]{:S(2)}) collective-permute-start(bf16[32,3072]{1,0:T(8,128)(2,1)S(1)} %get-tuple-element.22), channel_id=1, source_target_pairs={{0,1},{1,0},{2,3},{3,2},{4,5},{5,4},{6,7},{7,6},{8,9},{9,8},{10,11... | collective-permute-start | bytes 589832 | tf_op jit(solution)/shard_map/ppermute | solution.py:241
  36.7 4.2 %collective-permute-start.9 = (bf16[32,3072]{1,0:T(8,128)(2,1)S(1)}, bf16[32,3072]{1,0:T(8,128)(2,1)S(1)}, u32[]{:S(2)}, u32[]{:S(2)}) collective-permute-start(bf16[32,3072]{1,0:T(8,128)(2,1)S(1)} %get-tuple-element.20), channel_id=1, source_target_pairs={{0,1},{1,0},{2,3},{3,2},{4,5},{5,4},{6,7},{7,6},{8,9},{9,8},{10,11... | collective-permute-start | bytes 589832 | tf_op jit(solution)/shard_map/ppermute | solution.py:241
  37.2 7.0 %collective-permute-start.11 = (bf16[32,3072]{1,0:T(8,128)(2,1)S(1)}, bf16[32,3072]{1,0:T(8,128)(2,1)S(1)}, u32[]{:S(2)}, u32[]{:S(2)}) collective-permute-start(bf16[32,3072]{1,0:T(8,128)(2,1)S(1)} %add_convert_fusion), channel_id=1, source_target_pairs={{0,2},{1,3},{2,0},{3,1},{4,6},{5,7},{6,4},{7,5},{8,10},{9,11},{10,... | collective-permute-start | bytes 589832 | tf_op jit(solution)/shard_map/ppermute | solution.py:241

commit v2 on v1

v2 whole, which is shorter than its diff:
```python
import math

import jax
import jax.numpy as jnp
from jax import lax
from jax.experimental import pallas as pl
from jax.experimental.pallas import tpu as pltpu
from jax.sharding import PartitionSpec as P

HEAD_DIM = 128
MASKED = -1e30
VMEM = pl.BlockSpec(memory_space=pltpu.VMEM)
SMEM = pl.BlockSpec(memory_space=pltpu.SMEM)
ANY = pl.BlockSpec(memory_space=pl.ANY)


MIB = 1024 * 1024
SPLIT_ROOM, WEIGH_ROOM, PROJECT_ROOM = 8 * MIB, 46 * MIB, 32 * MIB


def params(room):
    return pltpu.CompilerParams(vmem_limit_bytes=room)


def padded(rows):
    return -(-rows // 128) * 128


def split_qkv(qkv_t, lengths, n_head, keep, origins):
    planes, tok_rows, width = qkv_t.shape
    columns = width // n_head
    rows = n_head * tok_rows
    pitch = padded(keep)
    blocks = len(origins(None, None))
    total = padded(rows) + blocks * pitch

    def kernel(src, lengths_ref, *rest):
        outs, live_ref, sems = rest[:n_head], rest[n_head], rest[n_head + 1]
        mine = lax.axis_index("head")
        patch = lax.axis_index("patch")
        copies = []
        for j in range(n_head):
            start = pl.multiple_of((mine ^ j) * columns, columns)
            copies.append(
                pltpu.make_async_copy(src.at[:, :, pl.ds(start, columns)], outs[j], sems.at[j])
            )
        for copy in copies:
            copy.start()
        column = lax.broadcasted_iota(jnp.int32, (8, padded(rows)), 1)
        absolute = ((column // tok_rows) ^ mine) * tok_rows + column % tok_rows
        live_ref[:, : padded(rows)] = jnp.where(
            (absolute < lengths_ref[patch]) & (column < rows), 1.0, 0.0
        )
        row = lax.broadcasted_iota(jnp.int32, (8, pitch), 1)
        for number, limit in enumerate(origins(lengths_ref, patch)):
            first = padded(rows) + number * pitch
            live_ref[:, first : first + pitch] = jnp.where(row < limit, 1.0, 0.0)
        for copy in copies:
            copy.wait()

    return pl.pallas_call(
        kernel,
        out_shape=[jax.ShapeDtypeStruct((planes, tok_rows, columns), qkv_t.dtype)] * n_head
        + [jax.ShapeDtypeStruct((8, total), jnp.float32)],
        in_specs=[ANY, SMEM],
        out_specs=[ANY] * n_head + [VMEM],
        scratch_shapes=[pltpu.SemaphoreType.DMA((n_head,))],
        compiler_params=params(SPLIT_ROOM),
    )(qkv_t, lengths)


def weigh(live, pieces, stale_keys, w_out):
    n_head = len(pieces)
    _, tok_rows, columns = pieces[0].shape
    rows = n_head * tok_rows
    heads = columns // HEAD_DIM
    keep = rows * 3 // 4
    per_array = [array.shape[1] // keep for array, _ in stale_keys]
    pitch = padded(keep)
    total = live.shape[1]
    scale = 1.0 / math.sqrt(HEAD_DIM)

    def kernel(live_ref, *rest):
        piece_refs = rest[:n_head]
        key_refs = rest[n_head : n_head + len(stale_keys)]
        rest = rest[n_head + len(stale_keys) :]
        w_ref, weights_ref, sums_ref, kv_ref, held_ref, query_buf, key_buf, sem = rest
        bring = pltpu.make_async_copy(w_ref, held_ref, sem)
        bring.start()
        mine = lax.axis_index("head")
        for j in range(n_head):
            here = pl.ds(j * tok_rows, tok_rows)
            query_buf[here, :] = piece_refs[j][0]
            key_buf[here, :] = piece_refs[j][1]
            there = pl.ds(pl.multiple_of((mine ^ j) * tok_rows, tok_rows), tok_rows)
            kv_ref[0, there, :] = piece_refs[j][1]
            kv_ref[1, there, :] = piece_refs[j][2]
        for head in range(heads):
            lanes = slice(head * HEAD_DIM, (head + 1) * HEAD_DIM)
            queries = query_buf[:, lanes]

            def score(keys, first):
                found = lax.dot_general(
                    queries, keys, (((1,), (1,)), ((), ())), preferred_element_type=jnp.float32
                )
                usable = live_ref[0:1, first : first + keys.shape[0]] > 0.5
                return jnp.where(usable, found * scale, MASKED)

            parts, firsts = [score(key_buf[:, lanes], 0)], [0]
            first = padded(rows)
            for ref, (_, plane), count in zip(key_refs, stale_keys, per_array):
                for block in range(count):
                    keys = ref[plane, block * keep : (block + 1) * keep, lanes]
                    parts.append(score(keys, first))
                    firsts.append(first)
                    first += pitch
            top = jnp.max(parts[0], axis=1, keepdims=True)
            for part in parts[1:]:
                top = jnp.maximum(top, jnp.max(part, axis=1, keepdims=True))
            weight_sum = jnp.zeros_like(top)
            for part, first in zip(parts, firsts):
                weights = jnp.exp(part - top)
                weight_sum = weight_sum + jnp.sum(weights, axis=1, keepdims=True)
                weights_ref[head, :, first : first + part.shape[1]] = weights.astype(jnp.bfloat16)
            sums_ref[head] = weight_sum
        bring.wait()

    return pl.pallas_call(
        kernel,
        out_shape=[
            jax.ShapeDtypeStruct((heads, rows, total), jnp.bfloat16),
            jax.ShapeDtypeStruct((heads, rows, 1), jnp.float32),
            jax.ShapeDtypeStruct((2, rows, columns), jnp.bfloat16),
            jax.ShapeDtypeStruct(w_out.shape, w_out.dtype),
        ],
        in_specs=[VMEM] * (1 + n_head + len(stale_keys)) + [ANY],
        out_specs=[VMEM] * 4,
        scratch_shapes=[
            pltpu.VMEM((rows, columns), jnp.bfloat16),
            pltpu.VMEM((rows, columns), jnp.bfloat16),
            pltpu.SemaphoreType.DMA,
        ],
        compiler_params=params(WEIGH_ROOM),
    )(live, *pieces, *[array for array, _ in stale_keys], w_out)


def project(weights, sums, pieces, stale_values, w_out, which):
    n_head = len(pieces)
    _, tok_rows, columns = pieces[0].shape
    rows = n_head * tok_rows
    heads = columns // HEAD_DIM
    keep = rows * 3 // 4
    per_array = [array.shape[1] // keep for array, _ in stale_values]
    pitch = padded(keep)
    model = w_out.shape[1]
    first_row, row_count = which[0] * tok_rows, len(which) * tok_rows

    def kernel(weights_ref, sums_ref, *rest):
        piece_refs = rest[:n_head]
        value_refs = rest[n_head : n_head + len(stale_values)]
        w_ref = rest[n_head + len(stale_values)]
        out_refs = rest[n_head + len(stale_values) + 1 : -2]
        value_buf, attended_buf = rest[-2:]
        here = slice(first_row, first_row + row_count)
        for j in range(n_head):
            value_buf[j * tok_rows : (j + 1) * tok_rows, :] = piece_refs[j][2]
        for head in range(heads):
            lanes = slice(head * HEAD_DIM, (head + 1) * HEAD_DIM)
            mixed = jnp.dot(
                weights_ref[head, here, :rows],
                value_buf[:, lanes],
                preferred_element_type=jnp.float32,
            )
            first = padded(rows)
            for ref, (_, plane), count in zip(value_refs, stale_values, per_array):
                for block in range(count):
                    mixed = mixed + jnp.dot(
                        weights_ref[head, here, first : first + keep],
                        ref[plane, block * keep : (block + 1) * keep, lanes],
                        preferred_element_type=jnp.float32,
                    )
                    first += pitch
            attended_buf[:, lanes] = (mixed / sums_ref[head, here, :]).astype(jnp.bfloat16)
        result = jnp.dot(attended_buf[...], w_ref[...], preferred_element_type=jnp.float32)
        for number, ref in enumerate(out_refs):
            ref[...] = result[number * tok_rows : (number + 1) * tok_rows].astype(ref.dtype)

    return pl.pallas_call(
        kernel,
        out_shape=[jax.ShapeDtypeStruct((tok_rows, model), jnp.bfloat16)] * len(which),
        in_specs=[VMEM] * (3 + n_head + len(stale_values)),
        out_specs=[VMEM] * len(which),
        scratch_shapes=[
            pltpu.VMEM((rows, columns), jnp.bfloat16),
            pltpu.VMEM((row_count, columns), jnp.bfloat16),
        ],
        compiler_params=params(PROJECT_ROOM),
    )(weights, sums, *pieces, *[array for array, _ in stale_values], w_out)


def add_pair(left, right):
    return (left.astype(jnp.float32) + right.astype(jnp.float32)).astype(jnp.bfloat16)


def build(n_head, n_patch):
    flip = [[(i, i ^ j) for i in range(n_head)] for j in range(n_head)]
    order = [0, 1, 3, 2]
    on_ring = n_patch == len(order)
    onward = [(order[i], order[(i + 1) % len(order)]) for i in range(len(order))]
    backward = [(b, a) for a, b in onward]

    def ring_limits(lengths_ref, patch):
        limits = []
        for back in (1, 3, 2):
            if lengths_ref is None:
                limits.append(None)
                continue
            origin = sum(jnp.where(patch == order[i], order[i - back], 0) for i in range(4))
            limits.append(lengths_ref[origin])
        return limits

    def gathered_limits(lengths_ref, patch):
        if lengths_ref is None:
            return [None] * n_patch
        return [jnp.where(patch == i, 0, lengths_ref[i]) for i in range(n_patch)]

    def shards(qkv, stale_kv, w_out, gate_table, lengths, timestep):
        keep = stale_kv.shape[0] * 3 // 4
        origins = ring_limits if on_ring else gathered_limits
        qkv_t = jnp.transpose(qkv, (1, 0, 2))
        *sent, live = split_qkv(qkv_t, lengths, n_head, keep, origins)
        stale = jnp.transpose(stale_kv[:keep], (1, 0, 2))
        if on_ring:
            key_before = lax.ppermute(stale[:1], "patch", onward)
            stale, live = lax.optimization_barrier((stale, live))
            value_before = lax.ppermute(stale[1:], "patch", onward)
            after = lax.ppermute(stale, "patch", backward)
            key_two = lax.ppermute(key_before, "patch", onward)
            value_two = lax.ppermute(value_before, "patch", onward)
            keys = [(key_before, 0), (after, 0), (key_two, 0)]
            values = [(value_before, 0), (after, 1), (value_two, 0)]
        else:
            gathered = lax.all_gather(stale, "patch", axis=1, tiled=True)
            keys, values = [(gathered, 0)], [(gathered, 1)]
        pieces = [sent[0]] + [lax.ppermute(sent[j], "head", flip[j]) for j in range(1, n_head)]
        weights, sums, next_t, w_held = weigh(live, pieces, keys, w_out)
        next_kv = jnp.transpose(next_t, (1, 0, 2))
        gate_row = lax.dynamic_slice_in_dim(gate_table, timestep[0], 1, 0)[0].astype(jnp.float32)

        def combine(held):
            bit = 1
            while len(held) > 1:
                arrived = [lax.ppermute(held[j], "head", flip[bit]) for j in range(1, len(held), 2)]
                held = [add_pair(held[2 * i], arrived[i]) for i in range(len(arrived))]
                bit *= 2
            return held[0]

        half = n_head // 2
        partial = project(weights, sums, pieces, values, w_held, range(n_head))
        arrived = lax.ppermute(combine(partial[half:]), "head", flip[half])
        near = combine(partial[:half])
        projected = near.astype(jnp.float32) + arrived.astype(jnp.float32)
        branch = (gate_row[None, :] * projected).astype(jnp.bfloat16)
        return (branch, next_kv)

    return shards


def solution(mesh):
    return jax.shard_map(
        build(mesh.shape["head"], mesh.shape["patch"]),
        mesh=mesh,
        in_specs=(
            P(("groups", "patch", "head"), None, None),
            P(("groups", "patch"), None, "head"),
            P("head", None),
            P(),
            P("groups"),
            P("groups"),
        ),
        out_specs=(P(("groups", "patch", "head"), None), P(("groups", "patch"), None, "head")),
        check_vma=False,
    )
```

time: 45.3 us -> 39.8 us (0.88)
  Pallas kernels: 9.07 us -> 4.15 us
  waiting for transfers between devices: 10.9 us -> 10.3 us
  starting transfers between devices: 17.5 us -> 18 us
    pallas_call x2 -> x1, Pallas kernels: 6.99 us -> 1.1 us  [project(): pl.pallas_call(kernel, out_shape=[jax.ShapeDtypeStruct((tok_rows, model),...]
    ppermute x3, waiting for transfers between devices: 2.63 us -> 0.01 us  [shards(): lax.ppermute(sent[j], 'head', flip[j])]
    ppermute x9 -> x8, waiting for transfers between devices: 8.3 us -> 10.3 us  [the longest x1 3.58 us: shards(): arrived = lax.ppermute(combine(partial[half:]), 'head', flip[half])]
    pallas_call x1, Pallas kernels: 0.13 us -> 0.7 us  [split_qkv(): pl.pallas_call(kernel, out_shape=[jax.ShapeDtypeStruct((planes, tok_rows,...]
    slice x1 -> x3, local copies, waits for them, and re-layouts: 1.56 us -> 1.19 us  [the longest x1 1.16 us: shards(): stale = jnp.transpose(stale_kv[:keep], (1, 0, 2))]
    ppermute x9 -> x8, starting transfers between devices: 15.6 us -> 15.9 us  [the longest x1 7.3 us: shards(): key_two = lax.ppermute(key_before, 'patch', onward)]
    unnamed x7 -> x6, local copies, waits for them, and re-layouts: 2.91 us -> 2.9 us
  transfers between devices with their start and end apart: 12 -> 11, of which waited for: 6 -> 6; matrix products, arithmetic and copies ran while one was open for 5% -> 8% of each run, Pallas kernels for 12% -> 6%
where the time goes in v2:
time: 39.8 us; the launch traced here: 39.5 us
  starting transfers between devices  18 us (45%)
  waiting for transfers between devices  10.3 us (26%)
  Pallas kernels  4.15 us (10%)
  local copies, waits for them, and re-layouts  4.08 us (10%)
  other arithmetic  1.62 us (4%)
  between operations  1.37 us (3%)
    ppermute x1, starting transfers between devices, shards(): key_two = lax.ppermute(key_before, 'patch', onward)  7.3 us
    ppermute x1, waiting for transfers between devices, shards(): arrived = lax.ppermute(combine(partial[half:]), 'head', flip[half])  3.58 us
    unnamed x6, local copies, waits for them, and re-layouts  2.9 us
    ppermute x1, starting transfers between devices, shards(): key_before = lax.ppermute(stale[:1], 'patch', onward)  2.64 us
    pallas_call x1, Pallas kernels, weigh(): pl.pallas_call(kernel, out_shape=[jax.ShapeDtypeStruct((heads, rows, tota...  2.36 us
    ppermute x1, waiting for transfers between devices, shards(): value_before = lax.ppermute(stale[1:], 'patch', onward)  2.12 us
    ppermute x3, starting transfers between devices, shards(): lax.ppermute(sent[j], 'head', flip[j])  2.01 us
    ppermute x1, waiting for transfers between devices, shards(): key_two = lax.ppermute(key_before, 'patch', onward)  1.69 us
  transfers between devices with their start and end apart: 11, of which 6 were waited for; matrix products, arithmetic and copies ran while one was open for 8% of the time, Pallas kernels for 6%

profile of v2, /device:TPU:0, one launch (start us, length us, event | category | flops | bytes accessed | tf_op | source)
XLA Modules:
  0.0 39.5 jit_solution(11888703348927477914)
XLA Ops:
  0.6 0.0 copy-start
  0.6 1.1 %copy-done = bf16[32,3,3072]{2,0,1:T(8,128)(2,1)S(1)} copy-done((bf16[32,3,3072]{2,0,1:T(8,128)(2,1)S(1)}, bf16[32,3,3072]{2,0,1:T(8,128)(2,1)}, u32[]{:S(2)}) %copy-start) | copy-done | bytes 589848
  1.7 0.0 copy-start.1
  1.7 0.7 %copy-done.1 = s32[4]{0:T(128)S(1)} copy-done((s32[4]{0:T(128)S(1)}, s32[4]{0:T(128)}, u32[]{:S(2)}) %copy-start.1) | copy-done | bytes 40
  2.4 0.7 %shard_map.77 = (bf16[3,32,768]{2,1,0:T(8,128)(2,1)S(1)}, bf16[3,32,768]{2,1,0:T(8,128)(2,1)S(1)}, bf16[3,32,768]{2,1,0:T(8,128)(2,1)S(1)}, bf16[3,32,768]{2,1,0:T(8,128)(2,1)S(1)}, f32[8,512]{1,0:T(8,128)S(1)}) custom-call(bf16[3,32,3072]{2,1,0:T(8,128)(2,1)S(1)} %bitcast.10, s32[4]{0:T(128)S(1)} %copy-done.1), custom_call_target="tpu_custom_call" | custom-call | tf_op jit(solution)/shard_map/pallas_call | solution.py:61
  3.1 0.5 %collective-permute-start = (bf16[3,32,768]{2,1,0:T(8,128)(2,1)S(1)}, bf16[3,32,768]{2,1,0:T(8,128)(2,1)S(1)}, u32[]{:S(2)}, u32[]{:S(2)}) collective-permute-start(bf16[3,32,768]{2,1,0:T(8,128)(2,1)S(1)} %get-tuple-element.20), channel_id=1, source_target_pairs={{0,1},{1,0},{2,3},{3,2},{4,5},{5,4},{6,7},{7,6},{8,9},{9,8},{10,11... | collective-permute-start | bytes 442376 | tf_op jit(solution)/shard_map/ppermute | solution.py:245
  3.6 1.2 %slice.9 = bf16[96,2,768]{2,1,0:T(2,128)(2,1)S(1)} slice(bf16[128,2,768]{2,1,0:T(2,128)(2,1)} %param.7), slice={[0:96], [0:2], [0:768]} | slice | bytes 589824 | tf_op jit(solution)/shard_map/slice | solution.py:232
  4.8 2.6 %collective-permute-start.3 = (bf16[1,96,768]{2,1,0:T(8,128)(2,1)S(1)}, bf16[1,96,768]{2,1,0:T(8,128)(2,1)S(1)}, u32[]{:S(2)}, u32[]{:S(2)}) collective-permute-start(bf16[1,96,768]{2,1,0:T(8,128)(2,1)S(1)} %slice.12), channel_id=1, source_target_pairs={{0,4},{4,12},{12,8},{8,0},{1,5},{5,13},{13,9},{9,1},{2,6},{6,14},{... | collective-permute-start | bytes 442376 | tf_op jit(solution)/shard_map/ppermute | solution.py:234
  7.4 1.1 %collective-permute-start.4 = (bf16[2,96,768]{2,1,0:T(8,128)(2,1)S(1)}, bf16[2,96,768]{2,1,0:T(8,128)(2,1)S(1)}, u32[]{:S(2)}, u32[]{:S(2)}) collective-permute-start(bf16[2,96,768]{2,1,0:T(8,128)(2,1)S(1)} %bitcast.13), channel_id=1, source_target_pairs={{4,0},{12,4},{8,12},{0,8},{5,1},{13,5},{9,13},{1,9},{6,2},{14,6},{... | collective-permute-start | bytes 884744 | tf_op jit(solution)/shard_map/ppermute | solution.py:237
  8.5 1.6 %collective-permute-start.6 = (bf16[1,96,768]{2,1,0:T(8,128)(2,1)S(1)}, bf16[1,96,768]{2,1,0:T(8,128)(2,1)S(1)}, u32[]{:S(2)}, u32[]{:S(2)}) collective-permute-start(bf16[1,96,768]{2,1,0:T(8,128)(2,1)S(1)} %slice.11), channel_id=1, source_target_pairs={{0,4},{4,12},{12,8},{8,0},{1,5},{5,13},{13,9},{9,1},{2,6},{6,14},{... | collective-permute-start | bytes 442376 | tf_op jit(solution)/shard_map/ppermute | solution.py:236
  10.1 1.5 %collective-permute-start.1 = (bf16[3,32,768]{2,1,0:T(8,128)(2,1)S(1)}, bf16[3,32,768]{2,1,0:T(8,128)(2,1)S(1)}, u32[]{:S(2)}, u32[]{:S(2)}) collective-permute-start(bf16[3,32,768]{2,1,0:T(8,128)(2,1)S(1)} %get-tuple-element.21), channel_id=1, source_target_pairs={{0,2},{1,3},{2,0},{3,1},{4,6},{5,7},{6,4},{7,5},{8,10},{9,11},{10,... | collective-permute-start | bytes 442376 | tf_op jit(solution)/shard_map/ppermute | solution.py:245
  11.6 0.0 collective-permute-done.rest_1_
  11.6 0.0 collective-permute-start.2
  11.6 1.7 %collective-permute-done.3.rest_4_ = bf16[1,96,768]{2,1,0:T(8,128)(2,1)S(1)} collective-permute-done((bf16[1,96,768]{2,1,0:T(8,128)(2,1)S(1)}, bf16[1,96,768]{2,1,0:T(8,128)(2,1)S(1)}, u32[]{:S(2)}, u32[]{:S(2)}) %collective-permute-start.3) | collective-permute-done | bytes 147488 | tf_op jit(solution)/shard_map/ppermute | solution.py:234
  13.3 7.3 %collective-permute-start.5 = (bf16[1,96,768]{2,1,0:T(8,128)(2,1)S(1)}, bf16[1,96,768]{2,1,0:T(8,128)(2,1)S(1)}, u32[]{:S(2)}, u32[]{:S(2)}) collective-permute-start(bf16[1,96,768]{2,1,0:T(8,128)(2,1)S(1)} %collective-permute-done.3.rest_4_), channel_id=1, source_target_pairs={{0,4},{4,12},{12,8},{8,0},{1,5},{5,13},{13,9},{9,1},{2,6},{6,14},{... | collective-permute-start | bytes 442376 | tf_op jit(solution)/shard_map/ppermute | solution.py:238
  20.6 2.1 %collective-permute-done.6.rest_4_ = bf16[1,96,768]{2,1,0:T(8,128)(2,1)S(1)} collective-permute-done((bf16[1,96,768]{2,1,0:T(8,128)(2,1)S(1)}, bf16[1,96,768]{2,1,0:T(8,128)(2,1)S(1)}, u32[]{:S(2)}, u32[]{:S(2)}) %collective-permute-start.6) | collective-permute-done | bytes 147488 | tf_op jit(solution)/shard_map/ppermute | solution.py:236
  22.7 1.3 %collective-permute-start.7 = (bf16[1,96,768]{2,1,0:T(8,128)(2,1)S(1)}, bf16[1,96,768]{2,1,0:T(8,128)(2,1)S(1)}, u32[]{:S(2)}, u32[]{:S(2)}) collective-permute-start(bf16[1,96,768]{2,1,0:T(8,128)(2,1)S(1)} %collective-permute-done.6.rest_4_), channel_id=1, source_target_pairs={{0,4},{4,12},{12,8},{8,0},{1,5},{5,13},{13,9},{9,1},{2,6},{6,14},{... | collective-permute-start | bytes 442376 | tf_op jit(solution)/shard_map/ppermute | solution.py:239
  23.9 0.0 collective-permute-done.1.rest_2_
  23.9 0.0 collective-permute-done.2.rest_3_
  23.9 0.0 collective-permute-done.4.rest_5_
  24.0 1.7 %collective-permute-done.5.rest_6_ = bf16[1,96,768]{2,1,0:T(8,128)(2,1)S(1)} collective-permute-done((bf16[1,96,768]{2,1,0:T(8,128)(2,1)S(1)}, bf16[1,96,768]{2,1,0:T(8,128)(2,1)S(1)}, u32[]{:S(2)}, u32[]{:S(2)}) %collective-permute-start.5) | collective-permute-done | bytes 147488 | tf_op jit(solution)/shard_map/ppermute | solution.py:238
  25.6 2.4 %shard_map.78 = (bf16[6,128,512]{2,1,0:T(8,128)(2,1)S(1)}, f32[6,128,1]{2,1,0:T(8,128)S(1)}, bf16[2,128,768]{2,1,0:T(8,128)(2,1)S(1)}, bf16[768,3072]{1,0:T(8,128)(2,1)S(1)}) custom-call(f32[8,512]{1,0:T(8,128)S(1)} %get-tuple-element.18.live_ref, bf16[3,32,768]{2,1,0:T(8,128)(2,1)S(1)} %get-tuple-element.19.rest_0_, ...), custom_call_target="tpu_custom_call" | custom-call | tf_op jit(solution)/shard_map/pallas_call | solution.py:128
  28.0 1.0 %collective-permute-done.7.rest_6_ = bf16[1,96,768]{2,1,0:T(8,128)(2,1)S(1)} collective-permute-done((bf16[1,96,768]{2,1,0:T(8,128)(2,1)S(1)}, bf16[1,96,768]{2,1,0:T(8,128)(2,1)S(1)}, u32[]{:S(2)}, u32[]{:S(2)}) %collective-permute-start.7) | collective-permute-done | bytes 147488 | tf_op jit(solution)/shard_map/ppermute | solution.py:239
  29.1 1.1 %shard_map.79 = (bf16[32,3072]{1,0:T(8,128)(2,1)S(1)}, bf16[32,3072]{1,0:T(8,128)(2,1)S(1)}, bf16[32,3072]{1,0:T(8,128)(2,1)S(1)}, bf16[32,3072]{1,0:T(8,128)(2,1)S(1)}) custom-call(bf16[6,128,512]{2,1,0:T(8,128)(2,1)S(1)} %get-tuple-element.24.weights_ref, f32[6,128,1]{2,1,0:T(8,128)S(1)} %get-tuple-element.25.sums_ref, ...), custom_call_target="tpu_custom_call" | custom-call | tf_op jit(solution)/shard_map/pallas_call | solution.py:188
  30.2 0.1 collective-permute-start.9
  30.9 0.6 %collective-permute-start.8 = (bf16[32,3072]{1,0:T(8,128)(2,1)S(1)}, bf16[32,3072]{1,0:T(8,128)(2,1)S(1)}, u32[]{:S(2)}, u32[]{:S(2)}) collective-permute-start(bf16[32,3072]{1,0:T(8,128)(2,1)S(1)} %get-tuple-element.28), channel_id=1, source_target_pairs={{0,1},{1,0},{2,3},{3,2},{4,5},{5,4},{6,7},{7,6},{8,9},{9,8},{10,11... | collective-permute-start | bytes 589832 | tf_op jit(solution)/shard_map/ppermute | solution.py:253
  31.5 0.2 collective-permute-done.9
  31.7 1.5 %collective-permute-start.10 = (bf16[32,3072]{1,0:T(8,128)(2,1)S(1)}, bf16[32,3072]{1,0:T(8,128)(2,1)S(1)}, u32[]{:S(2)}, u32[]{:S(2)}) collective-permute-start(bf16[32,3072]{1,0:T(8,128)(2,1)S(1)} %add_convert_fusion), channel_id=1, source_target_pairs={{0,2},{1,3},{2,0},{3,1},{4,6},{5,7},{6,4},{7,5},{8,10},{9,11},{10,... | collective-permute-start | bytes 589832 | tf_op jit(solution)/shard_map/ppermute | solution.py:260
  33.2 0.8 %dynamic-slice_convert_fusion = f32[1,3072]{1,0:T(1,128)S(1)} fusion(bf16[50,3072]{1,0:T(8,128)(2,1)} %param.9, s32[]{:T(128)S(6)} %select_n.3), kind=kLoop, calls=%fused_computation.4 | loop fusion | flops 3072 | bytes 18436 | tf_op jit(solution)/shard_map/mul | solution.py:263
  34.0 1.2 %copy.9 = bf16[128,2,768]{2,1,0:T(2,128)(2,1)} copy(bf16[128,2,768]{2,0,1:T(8,128)(2,1)S(1)} %bitcast.11) | data formatting | bytes 786432
  35.1 0.0 collective-permute-done.8
  35.1 3.6 %collective-permute-done.10 = bf16[32,3072]{1,0:T(8,128)(2,1)S(1)} collective-permute-done((bf16[32,3072]{1,0:T(8,128)(2,1)S(1)}, bf16[32,3072]{1,0:T(8,128)(2,1)S(1)}, u32[]{:S(2)}, u32[]{:S(2)}) %collective-permute-start.10) | collective-permute-done | bytes 196640 | tf_op jit(solution)/shard_map/ppermute | solution.py:260
  38.7 0.8 %multiply_convert_fusion = bf16[32,3072]{1,0:T(8,128)(2,1)} fusion(bf16[32,3072]{1,0:T(8,128)(2,1)S(1)} %collective-permute-done.10, bf16[32,3072]{1,0:T(8,128)(2,1)S(1)} %collective-permute-done.8, bf16[32,3072]{1,0:T(8,128)(2,1)S(1)} %get-tuple-element.27, f32[3072]{0:T(1024)S(1)} %bitcast.15), kind=kLoop, calls=%fused_computation | loop fusion | flops 884736 | bytes 798720 | tf_op jit(solution)/shard_map/convert_element_type | solution.py:263
  (4 shorter events, 0.1 us)
Async XLA Ops:
  0.6 1.1 %copy-start = (bf16[32,3,3072]{2,0,1:T(8,128)(2,1)S(1)}, bf16[32,3,3072]{2,0,1:T(8,128)(2,1)}, u32[]{:S(2)}) copy-start(bf16[32,3,3072]{2,0,1:T(8,128)(2,1)} %param.6) | copy-start | bytes 1769476
  1.7 0.7 %copy-start.1 = (s32[4]{0:T(128)S(1)}, s32[4]{0:T(128)}, u32[]{:S(2)}) copy-start(s32[4]{0:T(128)} %lengths_ref.1) | copy-start | bytes 52
  3.1 8.5 %collective-permute-start = (bf16[3,32,768]{2,1,0:T(8,128)(2,1)S(1)}, bf16[3,32,768]{2,1,0:T(8,128)(2,1)S(1)}, u32[]{:S(2)}, u32[]{:S(2)}) collective-permute-start(bf16[3,32,768]{2,1,0:T(8,128)(2,1)S(1)} %get-tuple-element.20), channel_id=1, source_target_pairs={{0,1},{1,0},{2,3},{3,2},{4,5},{5,4},{6,7},{7,6},{8,9},{9,8},{10,11... | collective-permute-start | bytes 442376 | tf_op jit(solution)/shard_map/ppermute | solution.py:245
  4.8 8.5 %collective-permute-start.3 = (bf16[1,96,768]{2,1,0:T(8,128)(2,1)S(1)}, bf16[1,96,768]{2,1,0:T(8,128)(2,1)S(1)}, u32[]{:S(2)}, u32[]{:S(2)}) collective-permute-start(bf16[1,96,768]{2,1,0:T(8,128)(2,1)S(1)} %slice.12), channel_id=1, source_target_pairs={{0,4},{4,12},{12,8},{8,0},{1,5},{5,13},{13,9},{9,1},{2,6},{6,14},{... | collective-permute-start | bytes 442376 | tf_op jit(solution)/shard_map/ppermute | solution.py:234
  7.4 16.5 %collective-permute-start.4 = (bf16[2,96,768]{2,1,0:T(8,128)(2,1)S(1)}, bf16[2,96,768]{2,1,0:T(8,128)(2,1)S(1)}, u32[]{:S(2)}, u32[]{:S(2)}) collective-permute-start(bf16[2,96,768]{2,1,0:T(8,128)(2,1)S(1)} %bitcast.13), channel_id=1, source_target_pairs={{4,0},{12,4},{8,12},{0,8},{5,1},{13,5},{9,13},{1,9},{6,2},{14,6},{... | collective-permute-start | bytes 884744 | tf_op jit(solution)/shard_map/ppermute | solution.py:237
  8.5 14.1 %collective-permute-start.6 = (bf16[1,96,768]{2,1,0:T(8,128)(2,1)S(1)}, bf16[1,96,768]{2,1,0:T(8,128)(2,1)S(1)}, u32[]{:S(2)}, u32[]{:S(2)}) collective-permute-start(bf16[1,96,768]{2,1,0:T(8,128)(2,1)S(1)} %slice.11), channel_id=1, source_target_pairs={{0,4},{4,12},{12,8},{8,0},{1,5},{5,13},{13,9},{9,1},{2,6},{6,14},{... | collective-permute-start | bytes 442376 | tf_op jit(solution)/shard_map/ppermute | solution.py:236
  10.1 13.8 %collective-permute-start.1 = (bf16[3,32,768]{2,1,0:T(8,128)(2,1)S(1)}, bf16[3,32,768]{2,1,0:T(8,128)(2,1)S(1)}, u32[]{:S(2)}, u32[]{:S(2)}) collective-permute-start(bf16[3,32,768]{2,1,0:T(8,128)(2,1)S(1)} %get-tuple-element.21), channel_id=1, source_target_pairs={{0,2},{1,3},{2,0},{3,1},{4,6},{5,7},{6,4},{7,5},{8,10},{9,11},{10,... | collective-permute-start | bytes 442376 | tf_op jit(solution)/shard_map/ppermute | solution.py:245
  11.6 12.3 %collective-permute-start.2 = (bf16[3,32,768]{2,1,0:T(8,128)(2,1)S(1)}, bf16[3,32,768]{2,1,0:T(8,128)(2,1)S(1)}, u32[]{:S(2)}, u32[]{:S(2)}) collective-permute-start(bf16[3,32,768]{2,1,0:T(8,128)(2,1)S(1)} %get-tuple-element.22), channel_id=1, source_target_pairs={{0,3},{1,2},{2,1},{3,0},{4,7},{5,6},{6,5},{7,4},{8,11},{9,10},{10,... | collective-permute-start | bytes 442376 | tf_op jit(solution)/shard_map/ppermute | solution.py:245
  13.3 12.4 %collective-permute-start.5 = (bf16[1,96,768]{2,1,0:T(8,128)(2,1)S(1)}, bf16[1,96,768]{2,1,0:T(8,128)(2,1)S(1)}, u32[]{:S(2)}, u32[]{:S(2)}) collective-permute-start(bf16[1,96,768]{2,1,0:T(8,128)(2,1)S(1)} %collective-permute-done.3.rest_4_), channel_id=1, source_target_pairs={{0,4},{4,12},{12,8},{8,0},{1,5},{5,13},{13,9},{9,1},{2,6},{6,14},{... | collective-permute-start | bytes 442376 | tf_op jit(solution)/shard_map/ppermute | solution.py:238
  22.7 6.4 %collective-permute-start.7 = (bf16[1,96,768]{2,1,0:T(8,128)(2,1)S(1)}, bf16[1,96,768]{2,1,0:T(8,128)(2,1)S(1)}, u32[]{:S(2)}, u32[]{:S(2)}) collective-permute-start(bf16[1,96,768]{2,1,0:T(8,128)(2,1)S(1)} %collective-permute-done.6.rest_4_), channel_id=1, source_target_pairs={{0,4},{4,12},{12,8},{8,0},{1,5},{5,13},{13,9},{9,1},{2,6},{6,14},{... | collective-permute-start | bytes 442376 | tf_op jit(solution)/shard_map/ppermute | solution.py:239
  30.2 1.5 %collective-permute-start.9 = (bf16[32,3072]{1,0:T(8,128)(2,1)S(1)}, bf16[32,3072]{1,0:T(8,128)(2,1)S(1)}, u32[]{:S(2)}, u32[]{:S(2)}) collective-permute-start(bf16[32,3072]{1,0:T(8,128)(2,1)S(1)} %get-tuple-element.30), channel_id=1, source_target_pairs={{0,1},{1,0},{2,3},{3,2},{4,5},{5,4},{6,7},{7,6},{8,9},{9,8},{10,11... | collective-permute-start | bytes 589832 | tf_op jit(solution)/shard_map/ppermute | solution.py:253
  30.9 4.3 %collective-permute-start.8 = (bf16[32,3072]{1,0:T(8,128)(2,1)S(1)}, bf16[32,3072]{1,0:T(8,128)(2,1)S(1)}, u32[]{:S(2)}, u32[]{:S(2)}) collective-permute-start(bf16[32,3072]{1,0:T(8,128)(2,1)S(1)} %get-tuple-element.28), channel_id=1, source_target_pairs={{0,1},{1,0},{2,3},{3,2},{4,5},{5,4},{6,7},{7,6},{8,9},{9,8},{10,11... | collective-permute-start | bytes 589832 | tf_op jit(solution)/shard_map/ppermute | solution.py:253
  31.7 7.0 %collective-permute-start.10 = (bf16[32,3072]{1,0:T(8,128)(2,1)S(1)}, bf16[32,3072]{1,0:T(8,128)(2,1)S(1)}, u32[]{:S(2)}, u32[]{:S(2)}) collective-permute-start(bf16[32,3072]{1,0:T(8,128)(2,1)S(1)} %add_convert_fusion), channel_id=1, source_target_pairs={{0,2},{1,3},{2,0},{3,1},{4,6},{5,7},{6,4},{7,5},{8,10},{9,11},{10,... | collective-permute-start | bytes 589832 | tf_op jit(solution)/shard_map/ppermute | solution.py:260

commit v3 on v2

--- a/solution.py
+++ b/solution.py
@@ -26,18 +26,13 @@
     return -(-rows // 128) * 128
 
 
-def split_qkv(qkv_t, lengths, n_head, keep, origins):
+def split_qkv(qkv_t, n_head):
     planes, tok_rows, width = qkv_t.shape
     columns = width // n_head
-    rows = n_head * tok_rows
-    pitch = padded(keep)
-    blocks = len(origins(None, None))
-    total = padded(rows) + blocks * pitch
-
-    def kernel(src, lengths_ref, *rest):
-        outs, live_ref, sems = rest[:n_head], rest[n_head], rest[n_head + 1]
+
+    def kernel(src, *rest):
+        outs, sems = rest[:n_head], rest[n_head]
         mine = lax.axis_index("head")
-        patch = lax.axis_index("patch")
         copies = []
         for j in range(n_head):
             start = pl.multiple_of((mine ^ j) * columns, columns)
@@ -46,27 +41,17 @@
             )
         for copy in copies:
             copy.start()
-        column = lax.broadcasted_iota(jnp.int32, (8, padded(rows)), 1)
-        absolute = ((column // tok_rows) ^ mine) * tok_rows + column % tok_rows
-        live_ref[:, : padded(rows)] = jnp.where(
-            (absolute < lengths_ref[patch]) & (column < rows), 1.0, 0.0
-        )
-        row = lax.broadcasted_iota(jnp.int32, (8, pitch), 1)
-        for number, limit in enumerate(origins(lengths_ref, patch)):
-            first = padded(rows) + number * pitch
-            live_ref[:, first : first + pitch] = jnp.where(row < limit, 1.0, 0.0)
         for copy in copies:
             copy.wait()
 
     return pl.pallas_call(
         kernel,
-        out_shape=[jax.ShapeDtypeStruct((planes, tok_rows, columns), qkv_t.dtype)] * n_head
-        + [jax.ShapeDtypeStruct((8, total), jnp.float32)],
-        in_specs=[ANY, SMEM],
-        out_specs=[ANY] * n_head + [VMEM],
+        out_shape=[jax.ShapeDtypeStruct((planes, tok_rows, columns), qkv_t.dtype)] * n_head,
+        in_specs=[ANY],
+        out_specs=[ANY] * n_head,
         scratch_shapes=[pltpu.SemaphoreType.DMA((n_head,))],
         compiler_params=params(SPLIT_ROOM),
-    )(qkv_t, lengths)
+    )(qkv_t)
 
 
 def weigh(live, pieces, stale_keys, w_out):
@@ -103,7 +88,7 @@
                 found = lax.dot_general(
                     queries, keys, (((1,), (1,)), ((), ())), preferred_element_type=jnp.float32
                 )
-                usable = live_ref[0:1, first : first + keys.shape[0]] > 0.5
+                usable = live_ref[0:1, first : first + keys.shape[0]] > 0
                 return jnp.where(usable, found * scale, MASKED)
 
             parts, firsts = [score(key_buf[:, lanes], 0)], [0]
@@ -209,30 +194,42 @@
     onward = [(order[i], order[(i + 1) % len(order)]) for i in range(len(order))]
     backward = [(b, a) for a, b in onward]
 
-    def ring_limits(lengths_ref, patch):
-        limits = []
-        for back in (1, 3, 2):
-            if lengths_ref is None:
-                limits.append(None)
-                continue
-            origin = sum(jnp.where(patch == order[i], order[i - back], 0) for i in range(4))
-            limits.append(lengths_ref[origin])
-        return limits
-
-    def gathered_limits(lengths_ref, patch):
-        if lengths_ref is None:
-            return [None] * n_patch
-        return [jnp.where(patch == i, 0, lengths_ref[i]) for i in range(n_patch)]
+    if on_ring:
+        sources = [[order[order.index(p) - back] for back in (1, 3, 2)] for p in range(n_patch)]
+    else:
+        sources = [[q if q != p else n_patch for q in range(n_patch)] for p in range(n_patch)]
+
+    def mark_live(lengths, tok_rows, keep):
+        rows, pitch = n_head * tok_rows, padded(keep)
+        owner, within = [], []
+        for p in range(n_patch):
+            owner.append([p] * rows + [n_patch] * (padded(rows) - rows))
+            for source in sources[p]:
+                owner[p] += [source] * keep + [n_patch] * (pitch - keep)
+        total = len(owner[0])
+        column = lax.broadcasted_iota(jnp.int32, (1, total), 1)
+        mine = lax.axis_index("head").astype(jnp.int32)
+        own = lax.dynamic_slice(
+            jnp.asarray(owner, jnp.int32),
+            (lax.axis_index("patch").astype(jnp.uint32), jnp.uint32(0)),
+            (1, total),
+        )
+        fresh = column ^ (mine * tok_rows)
+        within = jnp.where(column < padded(rows), fresh, (column - padded(rows)) % pitch)
+        patches = lax.broadcasted_iota(jnp.int32, (n_patch, total), 0)
+        found = (own == patches) & (within < lengths[:, None])
+        return jnp.sum(found.astype(jnp.int32), axis=0, keepdims=True)
 
     def shards(qkv, stale_kv, w_out, gate_table, lengths, timestep):
         keep = stale_kv.shape[0] * 3 // 4
-        origins = ring_limits if on_ring else gathered_limits
         qkv_t = jnp.transpose(qkv, (1, 0, 2))
-        *sent, live = split_qkv(qkv_t, lengths, n_head, keep, origins)
         stale = jnp.transpose(stale_kv[:keep], (1, 0, 2))
+        stale, qkv_t = lax.optimization_barrier((stale, qkv_t))
+        sent = split_qkv(qkv_t, n_head)
+        live = mark_live(lengths, qkv.shape[0], keep)
         if on_ring:
             key_before = lax.ppermute(stale[:1], "patch", onward)
-            stale, live = lax.optimization_barrier((stale, live))
+            key_before, _ = lax.optimization_barrier((key_before, sent[0]))
             value_before = lax.ppermute(stale[1:], "patch", onward)
             after = lax.ppermute(stale, "patch", backward)
             key_two = lax.ppermute(key_before, "patch", onward)
@@ -245,7 +242,10 @@
         pieces = [sent[0]] + [lax.ppermute(sent[j], "head", flip[j]) for j in range(1, n_head)]
         weights, sums, next_t, w_held = weigh(live, pieces, keys, w_out)
         next_kv = jnp.transpose(next_t, (1, 0, 2))
-        gate_row = lax.dynamic_slice_in_dim(gate_table, timestep[0], 1, 0)[0].astype(jnp.float32)
+        steps = lax.broadcasted_iota(jnp.int32, gate_table.shape, 0)
+        gate_row = jnp.sum(
+            jnp.where(steps == timestep[:, None], gate_table.astype(jnp.float32), 0.0), axis=0
+        )
 
         def combine(held):
             bit = 1

time: 39.8 us -> 37.5 us (0.942)
  starting transfers between devices: 18 us -> 13.6 us
  waiting for transfers between devices: 10.3 us -> 12.7 us
  Pallas kernels: 4.15 us -> 3.59 us
    ppermute x1, starting transfers between devices: 7.3 us -> 1.74 us  [shards(): key_two = lax.ppermute(key_before, 'patch', onward)]
    ppermute x1, waiting for transfers between devices: 1.69 us -> 6.7 us  [shards(): key_two = lax.ppermute(key_before, 'patch', onward)]
    ppermute x1, waiting for transfers between devices: 1.65 us -> 0.01 us  [shards(): key_before = lax.ppermute(stale[:1], 'patch', onward)]
    ppermute x1, waiting for transfers between devices: 2.12 us -> 1 us  [shards(): value_before = lax.ppermute(stale[1:], 'patch', onward)]
    ppermute x1, starting transfers between devices: 1.57 us -> 2.64 us  [shards(): value_before = lax.ppermute(stale[1:], 'patch', onward)]
    reduce_sum x0 -> x2, other arithmetic: none -> 0.9 us  [the longest x1 0.74 us: mark_live(): return jnp.sum(found.astype(jnp.int32), axis=0, keepdims=True)]
    mul x1 -> x0, other arithmetic: 0.81 us -> none  [shards(): branch = (gate_row[None, :] * projected).astype(jnp.bfloat16)]
    ppermute x1, starting transfers between devices: 1.08 us -> 0.34 us  [shards(): after = lax.ppermute(stale, 'patch', backward)]
  transfers between devices with their start and end apart: 11 -> 11, of which waited for: 6 -> 6; matrix products, arithmetic and copies ran while one was open for 8% -> 8% of each run, Pallas kernels for 6% -> 7%
where the time goes in v3:
time: 37.5 us; the launch traced here: 37.2 us
  starting transfers between devices  13.6 us (36%)
  waiting for transfers between devices  12.7 us (34%)
  local copies, waits for them, and re-layouts  4.14 us (11%)
  Pallas kernels  3.59 us (10%)
  other arithmetic  1.73 us (5%)
  between operations  1.38 us (4%)
    ppermute x1, waiting for transfers between devices, shards(): key_two = lax.ppermute(key_before, 'patch', onward)  6.7 us
    ppermute x1, waiting for transfers between devices, shards(): arrived = lax.ppermute(combine(partial[half:]), 'head', flip[half])  4.12 us
    ppermute x1, starting transfers between devices, shards(): key_before = lax.ppermute(stale[:1], 'patch', onward)  3.08 us
    ppermute x1, starting transfers between devices, shards(): value_before = lax.ppermute(stale[1:], 'patch', onward)  2.64 us
    pallas_call x1, Pallas kernels, weigh(): pl.pallas_call(kernel, out_shape=[jax.ShapeDtypeStruct((heads, rows, tota...  2.36 us
    unnamed x6, local copies, waits for them, and re-layouts  2.25 us
    ppermute x1, starting transfers between devices, shards(): value_two = lax.ppermute(value_before, 'patch', onward)  1.97 us
    ppermute x1, starting transfers between devices, shards(): key_two = lax.ppermute(key_before, 'patch', onward)  1.74 us
  transfers between devices with their start and end apart: 11, of which 6 were waited for; matrix products, arithmetic and copies ran while one was open for 8% of the time, Pallas kernels for 7%

profile of v3, /device:TPU:0, one launch (start us, length us, event | category | flops | bytes accessed | tf_op | source)
XLA Modules:
  0.0 37.2 jit_solution(1819755232877659162)
XLA Ops:
  0.6 1.2 %slice.9 = bf16[96,2,768]{2,1,0:T(2,128)(2,1)S(1)} slice(bf16[128,2,768]{2,1,0:T(2,128)(2,1)} %param.8), slice={[0:96], [0:2], [0:768]} | slice | bytes 589824 | tf_op jit(solution)/shard_map/slice | solution.py:226
  1.9 3.1 %collective-permute-start.3 = (bf16[1,96,768]{2,1,0:T(8,128)(2,1)S(1)}, bf16[1,96,768]{2,1,0:T(8,128)(2,1)S(1)}, u32[]{:S(2)}, u32[]{:S(2)}) collective-permute-start(bf16[1,96,768]{2,1,0:T(8,128)(2,1)S(1)} %get-tuple-element.37), channel_id=1, source_target_pairs={{0,4},{4,12},{12,8},{8,0},{1,5},{5,13},{13,9},{9,1},{2,6},{6,14},{... | collective-permute-start | bytes 442376 | tf_op jit(solution)/shard_map/ppermute | solution.py:231
  4.9 0.0 copy-start
  4.9 1.1 %copy-done = bf16[32,3,3072]{2,0,1:T(8,128)(2,1)S(1)} copy-done((bf16[32,3,3072]{2,0,1:T(8,128)(2,1)S(1)}, bf16[32,3,3072]{2,0,1:T(8,128)(2,1)}, u32[]{:S(2)}) %copy-start) | copy-done | bytes 589848
  6.0 0.1 shard_map.86
  6.1 0.1 collective-permute-start
  6.2 2.6 %collective-permute-start.6 = (bf16[1,96,768]{2,1,0:T(8,128)(2,1)S(1)}, bf16[1,96,768]{2,1,0:T(8,128)(2,1)S(1)}, u32[]{:S(2)}, u32[]{:S(2)}) collective-permute-start(bf16[1,96,768]{2,1,0:T(8,128)(2,1)S(1)} %get-tuple-element.36), channel_id=1, source_target_pairs={{0,4},{4,12},{12,8},{8,0},{1,5},{5,13},{13,9},{9,1},{2,6},{6,14},{... | collective-permute-start | bytes 442376 | tf_op jit(solution)/shard_map/ppermute | solution.py:233
  8.9 0.3 collective-permute-start.4
  9.2 1.5 %collective-permute-start.1 = (bf16[3,32,768]{2,1,0:T(8,128)(2,1)S(1)}, bf16[3,32,768]{2,1,0:T(8,128)(2,1)S(1)}, u32[]{:S(2)}, u32[]{:S(2)}) collective-permute-start(bf16[3,32,768]{2,1,0:T(8,128)(2,1)S(1)} %get-tuple-element.20), channel_id=1, source_target_pairs={{0,2},{1,3},{2,0},{3,1},{4,6},{5,7},{6,4},{7,5},{8,10},{9,11},{10,... | collective-permute-start | bytes 442376 | tf_op jit(solution)/shard_map/ppermute | solution.py:242
  10.7 0.0 collective-permute-done.3.rest_4_
  10.7 0.1 collective-permute-start.2
  10.8 0.0 collective-permute-done.rest_1_
  10.8 1.7 %collective-permute-start.5 = (bf16[1,96,768]{2,1,0:T(8,128)(2,1)S(1)}, bf16[1,96,768]{2,1,0:T(8,128)(2,1)S(1)}, u32[]{:S(2)}, u32[]{:S(2)}) collective-permute-start(bf16[1,96,768]{2,1,0:T(8,128)(2,1)S(1)} %collective-permute-done.3.rest_4_), channel_id=1, source_target_pairs={{0,4},{4,12},{12,8},{8,0},{1,5},{5,13},{13,9},{9,1},{2,6},{6,14},{... | collective-permute-start | bytes 442376 | tf_op jit(solution)/shard_map/ppermute | solution.py:235
  12.5 1.0 %collective-permute-done.6.rest_4_ = bf16[1,96,768]{2,1,0:T(8,128)(2,1)S(1)} collective-permute-done((bf16[1,96,768]{2,1,0:T(8,128)(2,1)S(1)}, bf16[1,96,768]{2,1,0:T(8,128)(2,1)S(1)}, u32[]{:S(2)}, u32[]{:S(2)}) %collective-permute-start.6) | collective-permute-done | bytes 147488 | tf_op jit(solution)/shard_map/ppermute | solution.py:233
  13.5 2.0 %collective-permute-start.7 = (bf16[1,96,768]{2,1,0:T(8,128)(2,1)S(1)}, bf16[1,96,768]{2,1,0:T(8,128)(2,1)S(1)}, u32[]{:S(2)}, u32[]{:S(2)}) collective-permute-start(bf16[1,96,768]{2,1,0:T(8,128)(2,1)S(1)} %collective-permute-done.6.rest_4_), channel_id=1, source_target_pairs={{0,4},{4,12},{12,8},{8,0},{1,5},{5,13},{13,9},{9,1},{2,6},{6,14},{... | collective-permute-start | bytes 442376 | tf_op jit(solution)/shard_map/ppermute | solution.py:236
  15.5 0.7 %constant_dynamic-slice_fusion = s32[1,512]{1,0:T(1,128)S(1)} fusion(s32[4,512]{1,0:T(4,128)} %constant.34.clone, u32[]{:T(128)S(6)} %convert_element_type.37), kind=kLoop, calls=%fused_computation.14 | loop fusion | bytes 4100 | tf_op jit(solution)/shard_map/dynamic_slice | solution.py:212
  16.2 0.7 %convert_reduce_fusion = s32[512]{0:T(512)S(1)} fusion(s32[512]{0:T(512)S(1)} %fusion.2, s32[512]{0:T(512)S(1)} %bitcast.14, s32[4]{0:T(128)} %param.11), kind=kLoop, calls=%fused_computation.5 | loop fusion | flops 9728 | bytes 6160 | tf_op jit(solution)/shard_map/reduce_sum | solution.py:221
  17.0 0.0 collective-permute-done.1.rest_2_
  17.0 0.1 collective-permute-done.2.rest_3_
  17.0 6.7 %collective-permute-done.5.rest_6_ = bf16[1,96,768]{2,1,0:T(8,128)(2,1)S(1)} collective-permute-done((bf16[1,96,768]{2,1,0:T(8,128)(2,1)S(1)}, bf16[1,96,768]{2,1,0:T(8,128)(2,1)S(1)}, u32[]{:S(2)}, u32[]{:S(2)}) %collective-permute-start.5) | collective-permute-done | bytes 147488 | tf_op jit(solution)/shard_map/ppermute | solution.py:235
  23.7 0.0 collective-permute-done.4.rest_5_
  23.7 2.4 %shard_map.87 = (bf16[6,128,512]{2,1,0:T(8,128)(2,1)S(1)}, f32[6,128,1]{2,1,0:T(8,128)S(1)}, bf16[2,128,768]{2,1,0:T(8,128)(2,1)S(1)}, bf16[768,3072]{1,0:T(8,128)(2,1)S(1)}) custom-call(s32[1,512]{1,0:T(1,128)S(1)} %bitcast.11, bf16[3,32,768]{2,1,0:T(8,128)(2,1)S(1)} %get-tuple-element.18.rest_0_, bf16[3,32,768]{2,1,0:T(8,128)(2,1)S(1)} %collective-permute-done.rest_1_, ...), custom_call_target="tpu_custom_call" | custom-call | tf_op jit(solution)/shard_map/pallas_call | solution.py:113
  26.1 0.0 copy-start.1
  26.1 0.6 %collective-permute-done.7.rest_6_ = bf16[1,96,768]{2,1,0:T(8,128)(2,1)S(1)} collective-permute-done((bf16[1,96,768]{2,1,0:T(8,128)(2,1)S(1)}, bf16[1,96,768]{2,1,0:T(8,128)(2,1)S(1)}, u32[]{:S(2)}, u32[]{:S(2)}) %collective-permute-start.7) | collective-permute-done | bytes 147488 | tf_op jit(solution)/shard_map/ppermute | solution.py:236
  26.7 1.1 %shard_map.88 = (bf16[32,3072]{1,0:T(8,128)(2,1)S(1)}, bf16[32,3072]{1,0:T(8,128)(2,1)S(1)}, bf16[32,3072]{1,0:T(8,128)(2,1)S(1)}, bf16[32,3072]{1,0:T(8,128)(2,1)S(1)}) custom-call(bf16[6,128,512]{2,1,0:T(8,128)(2,1)S(1)} %get-tuple-element.24.weights_ref, f32[6,128,1]{2,1,0:T(8,128)S(1)} %get-tuple-element.25.sums_ref, ...), custom_call_target="tpu_custom_call" | custom-call | tf_op jit(solution)/shard_map/pallas_call | solution.py:173
  27.8 0.1 collective-permute-start.9
  28.6 0.6 %collective-permute-start.8 = (bf16[32,3072]{1,0:T(8,128)(2,1)S(1)}, bf16[32,3072]{1,0:T(8,128)(2,1)S(1)}, u32[]{:S(2)}, u32[]{:S(2)}) collective-permute-start(bf16[32,3072]{1,0:T(8,128)(2,1)S(1)} %get-tuple-element.28), channel_id=1, source_target_pairs={{0,1},{1,0},{2,3},{3,2},{4,5},{5,4},{6,7},{7,6},{8,9},{9,8},{10,11... | collective-permute-start | bytes 589832 | tf_op jit(solution)/shard_map/ppermute | solution.py:253
  29.1 0.2 collective-permute-done.9
  29.4 1.6 %collective-permute-start.10 = (bf16[32,3072]{1,0:T(8,128)(2,1)S(1)}, bf16[32,3072]{1,0:T(8,128)(2,1)S(1)}, u32[]{:S(2)}, u32[]{:S(2)}) collective-permute-start(bf16[32,3072]{1,0:T(8,128)(2,1)S(1)} %add_convert_fusion), channel_id=1, source_target_pairs={{0,2},{1,3},{2,0},{3,1},{4,6},{5,7},{6,4},{7,5},{8,10},{9,11},{10,... | collective-permute-start | bytes 589832 | tf_op jit(solution)/shard_map/ppermute | solution.py:260
  31.0 0.0 copy-done.1
  31.0 0.2 select_reduce_fusion
  31.1 1.2 %copy.12 = bf16[128,2,768]{2,1,0:T(2,128)(2,1)} copy(bf16[128,2,768]{2,0,1:T(8,128)(2,1)S(1)} %bitcast.10) | data formatting | bytes 786432
  32.3 0.0 collective-permute-done.8
  32.3 4.1 %collective-permute-done.10 = bf16[32,3072]{1,0:T(8,128)(2,1)S(1)} collective-permute-done((bf16[32,3072]{1,0:T(8,128)(2,1)S(1)}, bf16[32,3072]{1,0:T(8,128)(2,1)S(1)}, u32[]{:S(2)}, u32[]{:S(2)}) %collective-permute-start.10) | collective-permute-done | bytes 196640 | tf_op jit(solution)/shard_map/ppermute | solution.py:260
  36.4 0.8 %multiply_convert_fusion = bf16[32,3072]{1,0:T(8,128)(2,1)} fusion(bf16[32,3072]{1,0:T(8,128)(2,1)S(1)} %collective-permute-done.10, bf16[32,3072]{1,0:T(8,128)(2,1)S(1)} %collective-permute-done.8, bf16[32,3072]{1,0:T(8,128)(2,1)S(1)} %get-tuple-element.27, f32[3072]{0:T(1024)S(1)} %select_reduce_fusion), kind=kLoop, calls=%fused_computation.1 | loop fusion | flops 884736 | bytes 798720 | tf_op jit(solution)/shard_map/convert_element_type | solution.py:263
  (5 shorter events, 0.1 us)
Async XLA Ops:
  1.9 8.8 %collective-permute-start.3 = (bf16[1,96,768]{2,1,0:T(8,128)(2,1)S(1)}, bf16[1,96,768]{2,1,0:T(8,128)(2,1)S(1)}, u32[]{:S(2)}, u32[]{:S(2)}) collective-permute-start(bf16[1,96,768]{2,1,0:T(8,128)(2,1)S(1)} %get-tuple-element.37), channel_id=1, source_target_pairs={{0,4},{4,12},{12,8},{8,0},{1,5},{5,13},{13,9},{9,1},{2,6},{6,14},{... | collective-permute-start | bytes 442376 | tf_op jit(solution)/shard_map/ppermute | solution.py:231
  4.9 1.1 %copy-start = (bf16[32,3,3072]{2,0,1:T(8,128)(2,1)S(1)}, bf16[32,3,3072]{2,0,1:T(8,128)(2,1)}, u32[]{:S(2)}) copy-start(bf16[32,3,3072]{2,0,1:T(8,128)(2,1)} %param.7) | copy-start | bytes 1769476
  6.1 4.6 %collective-permute-start = (bf16[3,32,768]{2,1,0:T(8,128)(2,1)S(1)}, bf16[3,32,768]{2,1,0:T(8,128)(2,1)S(1)}, u32[]{:S(2)}, u32[]{:S(2)}) collective-permute-start(bf16[3,32,768]{2,1,0:T(8,128)(2,1)S(1)} %get-tuple-element.19), channel_id=1, source_target_pairs={{0,1},{1,0},{2,3},{3,2},{4,5},{5,4},{6,7},{7,6},{8,9},{9,8},{10,11... | collective-permute-start | bytes 442376 | tf_op jit(solution)/shard_map/ppermute | solution.py:242
  6.2 7.3 %collective-permute-start.6 = (bf16[1,96,768]{2,1,0:T(8,128)(2,1)S(1)}, bf16[1,96,768]{2,1,0:T(8,128)(2,1)S(1)}, u32[]{:S(2)}, u32[]{:S(2)}) collective-permute-start(bf16[1,96,768]{2,1,0:T(8,128)(2,1)S(1)} %get-tuple-element.36), channel_id=1, source_target_pairs={{0,4},{4,12},{12,8},{8,0},{1,5},{5,13},{13,9},{9,1},{2,6},{6,14},{... | collective-permute-start | bytes 442376 | tf_op jit(solution)/shard_map/ppermute | solution.py:233
  8.9 14.9 %collective-permute-start.4 = (bf16[2,96,768]{2,1,0:T(8,128)(2,1)S(1)}, bf16[2,96,768]{2,1,0:T(8,128)(2,1)S(1)}, u32[]{:S(2)}, u32[]{:S(2)}) collective-permute-start(bf16[2,96,768]{2,1,0:T(8,128)(2,1)S(1)} %bitcast.13), channel_id=1, source_target_pairs={{4,0},{12,4},{8,12},{0,8},{5,1},{13,5},{9,13},{1,9},{6,2},{14,6},{... | collective-permute-start | bytes 884744 | tf_op jit(solution)/shard_map/ppermute | solution.py:234
  9.2 7.8 %collective-permute-start.1 = (bf16[3,32,768]{2,1,0:T(8,128)(2,1)S(1)}, bf16[3,32,768]{2,1,0:T(8,128)(2,1)S(1)}, u32[]{:S(2)}, u32[]{:S(2)}) collective-permute-start(bf16[3,32,768]{2,1,0:T(8,128)(2,1)S(1)} %get-tuple-element.20), channel_id=1, source_target_pairs={{0,2},{1,3},{2,0},{3,1},{4,6},{5,7},{6,4},{7,5},{8,10},{9,11},{10,... | collective-permute-start | bytes 442376 | tf_op jit(solution)/shard_map/ppermute | solution.py:242
  10.7 6.3 %collective-permute-start.2 = (bf16[3,32,768]{2,1,0:T(8,128)(2,1)S(1)}, bf16[3,32,768]{2,1,0:T(8,128)(2,1)S(1)}, u32[]{:S(2)}, u32[]{:S(2)}) collective-permute-start(bf16[3,32,768]{2,1,0:T(8,128)(2,1)S(1)} %get-tuple-element.21), channel_id=1, source_target_pairs={{0,3},{1,2},{2,1},{3,0},{4,7},{5,6},{6,5},{7,4},{8,11},{9,10},{10,... | collective-permute-start | bytes 442376 | tf_op jit(solution)/shard_map/ppermute | solution.py:242
  10.8 12.9 %collective-permute-start.5 = (bf16[1,96,768]{2,1,0:T(8,128)(2,1)S(1)}, bf16[1,96,768]{2,1,0:T(8,128)(2,1)S(1)}, u32[]{:S(2)}, u32[]{:S(2)}) collective-permute-start(bf16[1,96,768]{2,1,0:T(8,128)(2,1)S(1)} %collective-permute-done.3.rest_4_), channel_id=1, source_target_pairs={{0,4},{4,12},{12,8},{8,0},{1,5},{5,13},{13,9},{9,1},{2,6},{6,14},{... | collective-permute-start | bytes 442376 | tf_op jit(solution)/shard_map/ppermute | solution.py:235
  13.5 13.2 %collective-permute-start.7 = (bf16[1,96,768]{2,1,0:T(8,128)(2,1)S(1)}, bf16[1,96,768]{2,1,0:T(8,128)(2,1)S(1)}, u32[]{:S(2)}, u32[]{:S(2)}) collective-permute-start(bf16[1,96,768]{2,1,0:T(8,128)(2,1)S(1)} %collective-permute-done.6.rest_4_), channel_id=1, source_target_pairs={{0,4},{4,12},{12,8},{8,0},{1,5},{5,13},{13,9},{9,1},{2,6},{6,14},{... | collective-permute-start | bytes 442376 | tf_op jit(solution)/shard_map/ppermute | solution.py:236
  26.1 4.9 %copy-start.1 = (bf16[50,3072]{1,0:T(8,128)(2,1)S(1)}, bf16[50,3072]{1,0:T(8,128)(2,1)}, u32[]{:S(2)}) copy-start(bf16[50,3072]{1,0:T(8,128)(2,1)} %param.10) | copy-start | bytes 921604
  27.8 1.5 %collective-permute-start.9 = (bf16[32,3072]{1,0:T(8,128)(2,1)S(1)}, bf16[32,3072]{1,0:T(8,128)(2,1)S(1)}, u32[]{:S(2)}, u32[]{:S(2)}) collective-permute-start(bf16[32,3072]{1,0:T(8,128)(2,1)S(1)} %get-tuple-element.30), channel_id=1, source_target_pairs={{0,1},{1,0},{2,3},{3,2},{4,5},{5,4},{6,7},{7,6},{8,9},{9,8},{10,11... | collective-permute-start | bytes 589832 | tf_op jit(solution)/shard_map/ppermute | solution.py:253
  28.6 3.7 %collective-permute-start.8 = (bf16[32,3072]{1,0:T(8,128)(2,1)S(1)}, bf16[32,3072]{1,0:T(8,128)(2,1)S(1)}, u32[]{:S(2)}, u32[]{:S(2)}) collective-permute-start(bf16[32,3072]{1,0:T(8,128)(2,1)S(1)} %get-tuple-element.28), channel_id=1, source_target_pairs={{0,1},{1,0},{2,3},{3,2},{4,5},{5,4},{6,7},{7,6},{8,9},{9,8},{10,11... | collective-permute-start | bytes 589832 | tf_op jit(solution)/shard_map/ppermute | solution.py:253
  29.4 7.0 %collective-permute-start.10 = (bf16[32,3072]{1,0:T(8,128)(2,1)S(1)}, bf16[32,3072]{1,0:T(8,128)(2,1)S(1)}, u32[]{:S(2)}, u32[]{:S(2)}) collective-permute-start(bf16[32,3072]{1,0:T(8,128)(2,1)S(1)} %add_convert_fusion), channel_id=1, source_target_pairs={{0,2},{1,3},{2,0},{3,1},{4,6},{5,7},{6,4},{7,5},{8,10},{9,11},{10,... | collective-permute-start | bytes 589832 | tf_op jit(solution)/shard_map/ppermute | solution.py:260

commit v4 on v3

v4 whole, which is shorter than its diff:
```python
import math

import jax
import jax.numpy as jnp
from jax import lax
from jax.experimental import pallas as pl
from jax.experimental.pallas import tpu as pltpu
from jax.sharding import PartitionSpec as P

HEAD_DIM = 128
MASKED = -1e30
VMEM = pl.BlockSpec(memory_space=pltpu.VMEM)
SMEM = pl.BlockSpec(memory_space=pltpu.SMEM)
ANY = pl.BlockSpec(memory_space=pl.ANY)


MIB = 1024 * 1024
SPLIT_ROOM, WEIGH_ROOM, PROJECT_ROOM = 8 * MIB, 46 * MIB, 32 * MIB

HALVES = 2


def params(room):
    return pltpu.CompilerParams(vmem_limit_bytes=room)


def padded(rows):
    return -(-rows // 128) * 128


def split_qkv(qkv_t, n_head):
    planes, tok_rows, width = qkv_t.shape
    columns = width // n_head

    def kernel(src, *rest):
        outs, sems = rest[:n_head], rest[n_head]
        mine = lax.axis_index("head")
        copies = []
        for j in range(n_head):
            start = pl.multiple_of((mine ^ j) * columns, columns)
            copies.append(
                pltpu.make_async_copy(src.at[:, :, pl.ds(start, columns)], outs[j], sems.at[j])
            )
        for copy in copies:
            copy.start()
        for copy in copies:
            copy.wait()

    return pl.pallas_call(
        kernel,
        out_shape=[jax.ShapeDtypeStruct((planes, tok_rows, columns), qkv_t.dtype)] * n_head,
        in_specs=[ANY],
        out_specs=[ANY] * n_head,
        scratch_shapes=[pltpu.SemaphoreType.DMA((n_head,))],
        compiler_params=params(SPLIT_ROOM),
    )(qkv_t)


def weigh(live, pieces, stale_keys, early_values, w_out):
    n_head = len(pieces)
    _, tok_rows, columns = pieces[0].shape
    rows = n_head * tok_rows
    heads = columns // HEAD_DIM
    keep = rows * 3 // 4
    pitch = padded(keep)
    n_keys, n_values = len(stale_keys), len(early_values)
    per_array = [array.shape[1] // keep for array, _ in stale_keys]
    late_blocks = sum(per_array[n_values:])
    scale = 1.0 / math.sqrt(HEAD_DIM)

    def kernel(live_ref, *rest):
        piece_refs, rest = rest[:n_head], rest[n_head:]
        key_refs, rest = rest[:n_keys], rest[n_keys:]
        value_refs, rest = rest[:n_values], rest[n_values:]
        w_ref, weights_ref, mixed_ref, sums_ref, kv_ref, held_ref, *rest = rest
        query_buf, key_buf, value_buf, sem = rest
        bring = pltpu.make_async_copy(w_ref, held_ref, sem)
        bring.start()
        mine = lax.axis_index("head")
        for j in range(n_head):
            here = pl.ds(j * tok_rows, tok_rows)
            query_buf[here, :] = piece_refs[j][0]
            key_buf[here, :] = piece_refs[j][1]
            value_buf[here, :] = piece_refs[j][2]
            there = pl.ds(pl.multiple_of((mine ^ j) * tok_rows, tok_rows), tok_rows)
            kv_ref[0, there, :] = piece_refs[j][1]
            kv_ref[1, there, :] = piece_refs[j][2]
        for head in range(heads):
            lanes = slice(head * HEAD_DIM, (head + 1) * HEAD_DIM)
            queries = query_buf[:, lanes]

            def score(keys, first):
                found = lax.dot_general(
                    queries, keys, (((1,), (1,)), ((), ())), preferred_element_type=jnp.float32
                )
                usable = live_ref[0:1, first : first + keys.shape[0]] > 0
                return jnp.where(usable, found * scale, MASKED)

            parts, values = [score(key_buf[:, lanes], 0)], [value_buf[:, lanes]]
            first = padded(rows)
            for number, (_, plane) in enumerate(stale_keys):
                for block in range(per_array[number]):
                    slots = slice(block * keep, (block + 1) * keep)
                    parts.append(score(key_refs[number][plane, slots, lanes], first))
                    first += pitch
                    if number < n_values:
                        values.append(value_refs[number][early_values[number][1], slots, lanes])
            top = jnp.max(parts[0], axis=1, keepdims=True)
            for part in parts[1:]:
                top = jnp.maximum(top, jnp.max(part, axis=1, keepdims=True))
            weight_sum = jnp.zeros_like(top)
            mixed = jnp.zeros((rows, HEAD_DIM), jnp.float32)
            for number, part in enumerate(parts):
                weights = jnp.exp(part - top)
                weight_sum = weight_sum + jnp.sum(weights, axis=1, keepdims=True)
                rounded = weights.astype(jnp.bfloat16)
                if number < len(values):
                    mixed = mixed + jnp.dot(
                        rounded, values[number], preferred_element_type=jnp.float32
                    )
                else:
                    first = (number - len(values)) * pitch
                    weights_ref[head, :, first : first + keep] = rounded
            mixed_ref[:, lanes] = mixed
            sums_ref[head] = weight_sum
        bring.wait()

    return pl.pallas_call(
        kernel,
        out_shape=[
            jax.ShapeDtypeStruct((heads, rows, late_blocks * pitch), jnp.bfloat16),
            jax.ShapeDtypeStruct((rows, columns), jnp.float32),
            jax.ShapeDtypeStruct((heads, rows, 1), jnp.float32),
            jax.ShapeDtypeStruct((2, rows, columns), jnp.bfloat16),
            jax.ShapeDtypeStruct(w_out.shape, w_out.dtype),
        ],
        in_specs=[VMEM] * (1 + n_head + n_keys + n_values) + [ANY],
        out_specs=[VMEM] * 5,
        scratch_shapes=[pltpu.VMEM((rows, columns), jnp.bfloat16)] * 3
        + [pltpu.SemaphoreType.DMA],
        compiler_params=params(WEIGH_ROOM),
    )(
        live,
        *pieces,
        *[array for array, _ in stale_keys],
        *[array for array, _ in early_values],
        w_out,
    )


def project(weights, mixed, sums, late_values, w_out, cuts):
    rows, columns = mixed.shape
    heads = columns // HEAD_DIM
    keep = rows * 3 // 4
    pitch = padded(keep)
    model = w_out.shape[1]
    n_values = len(late_values)

    def kernel(weights_ref, mixed_ref, sums_ref, *rest):
        value_refs, w_ref, out_refs = rest[:n_values], rest[n_values], rest[n_values + 1 : -1]
        attended_buf = rest[-1]
        for head in range(heads):
            lanes = slice(head * HEAD_DIM, (head + 1) * HEAD_DIM)
            total = mixed_ref[:, lanes]
            first = 0
            for ref, (array, plane) in zip(value_refs, late_values):
                for block in range(array.shape[1] // keep):
                    total = total + jnp.dot(
                        weights_ref[head, :, first : first + keep],
                        ref[plane, block * keep : (block + 1) * keep, lanes],
                        preferred_element_type=jnp.float32,
                    )
                    first += pitch
            attended_buf[:, lanes] = (total / sums_ref[head]).astype(jnp.bfloat16)
        result = jnp.dot(attended_buf[...], w_ref[...], preferred_element_type=jnp.float32)
        for (start, stop), ref in zip(cuts, out_refs):
            ref[...] = result[start:stop].astype(ref.dtype)

    return pl.pallas_call(
        kernel,
        out_shape=[jax.ShapeDtypeStruct((stop - start, model), jnp.bfloat16) for start, stop in cuts],
        in_specs=[VMEM] * (4 + n_values),
        out_specs=[VMEM] * len(cuts),
        scratch_shapes=[pltpu.VMEM((rows, columns), jnp.bfloat16)],
        compiler_params=params(PROJECT_ROOM),
    )(weights, mixed, sums, *[array for array, _ in late_values], w_out)


def finish(near, arrived, gate_row):
    def kernel(gate_ref, *rest):
        near_refs, arrived_refs, out_ref = rest[: len(near)], rest[len(near) : -1], rest[-1]
        start = 0
        for ref in arrived_refs:
            here = slice(start, start + ref.shape[0])
            total = ref[...].astype(jnp.float32)
            for near_ref in near_refs:
                total = total + near_ref[here].astype(jnp.float32)
            out_ref[here] = (gate_ref[...] * total).astype(out_ref.dtype)
            start += ref.shape[0]

    return pl.pallas_call(
        kernel,
        out_shape=jax.ShapeDtypeStruct(near[0].shape, near[0].dtype),
        in_specs=[VMEM] * (1 + len(near) + len(arrived)),
        out_specs=VMEM,
        compiler_params=params(PROJECT_ROOM),
    )(gate_row, *near, *arrived)


def add_pair(left, right):
    return (left.astype(jnp.float32) + right.astype(jnp.float32)).astype(jnp.bfloat16)


def build(n_head, n_patch):
    flip = [[(i, i ^ j) for i in range(n_head)] for j in range(n_head)]
    order = [0, 1, 3, 2]
    on_ring = n_patch == len(order)
    onward = [(order[i], order[(i + 1) % len(order)]) for i in range(len(order))]
    backward = [(b, a) for a, b in onward]

    if on_ring:
        sources = [[order[order.index(p) - back] for back in (1, 3, 2)] for p in range(n_patch)]
    else:
        sources = [[q if q != p else n_patch for q in range(n_patch)] for p in range(n_patch)]

    def mark_live(lengths, tok_rows, keep):
        rows, pitch = n_head * tok_rows, padded(keep)
        owner, within = [], []
        for p in range(n_patch):
            owner.append([p] * rows + [n_patch] * (padded(rows) - rows))
            for source in sources[p]:
                owner[p] += [source] * keep + [n_patch] * (pitch - keep)
        total = len(owner[0])
        column = lax.broadcasted_iota(jnp.int32, (1, total), 1)
        mine = lax.axis_index("head").astype(jnp.int32)
        own = lax.dynamic_slice(
            jnp.asarray(owner, jnp.int32),
            (lax.axis_index("patch").astype(jnp.uint32), jnp.uint32(0)),
            (1, total),
        )
        fresh = column ^ (mine * tok_rows)
        within = jnp.where(column < padded(rows), fresh, (column - padded(rows)) % pitch)
        patches = lax.broadcasted_iota(jnp.int32, (n_patch, total), 0)
        found = (own == patches) & (within < lengths[:, None])
        return jnp.sum(found.astype(jnp.int32), axis=0, keepdims=True)

    def shards(qkv, stale_kv, w_out, gate_table, lengths, timestep):
        keep = stale_kv.shape[0] * 3 // 4
        qkv_t = jnp.transpose(qkv, (1, 0, 2))
        stale = jnp.transpose(stale_kv[:keep], (1, 0, 2))
        stale, qkv_t = lax.optimization_barrier((stale, qkv_t))
        sent = list(split_qkv(qkv_t, n_head))
        live = mark_live(lengths, qkv.shape[0], keep)
        if on_ring:
            key_before = lax.ppermute(stale[:1], "patch", onward)
            value_before = lax.ppermute(stale[1:], "patch", onward)
            key_before, *sent[2:] = lax.optimization_barrier((key_before, *sent[2:]))
            both, _ = lax.optimization_barrier((stale, sent[0]))
            after = lax.ppermute(both, "patch", backward)
            key_two = lax.ppermute(key_before, "patch", onward)
            value_two = lax.ppermute(value_before, "patch", onward)
            keys = [(key_before, 0), (after, 0), (key_two, 0)]
            values = [(value_before, 0), (after, 1), (value_two, 0)]
        else:
            gathered = lax.all_gather(stale, "patch", axis=1, tiled=True)
            keys, values = [(gathered, 0)], [(gathered, 1)]
        pieces = [sent[0]] + [lax.ppermute(sent[j], "head", flip[j]) for j in range(1, n_head)]
        early = len(values) - 1
        weights, mixed, sums, next_t, w_held = weigh(live, pieces, keys, values[:early], w_out)
        steps = lax.broadcasted_iota(jnp.int32, gate_table.shape, 0)
        gate_row = jnp.sum(
            jnp.where(steps == timestep[:, None], gate_table.astype(jnp.float32), 0.0), axis=0, keepdims=True
        )

        def exchange(held):
            bit = 1
            while True:
                arrived = [lax.ppermute(held[j], "head", flip[bit]) for j in range(1, len(held), 2)]
                if len(arrived) == 1:
                    return held[0], arrived[0]
                held = [add_pair(held[2 * i], arrived[i]) for i in range(len(arrived))]
                bit *= 2

        half = n_head // 2
        tok_rows = qkv.shape[0]
        cut = tok_rows // HALVES
        near_cuts = [(j * tok_rows, (j + 1) * tok_rows) for j in range(half)]
        far_cuts = [
            (j * tok_rows + i * cut, j * tok_rows + (i + 1) * cut)
            for i in range(HALVES)
            for j in range(half, n_head)
        ]
        partial = project(weights, mixed, sums, values[early:], w_held, far_cuts + near_cuts)
        arrived = [
            lax.ppermute(add_pair(*exchange(partial[i * half : (i + 1) * half])), "head", flip[half])
            for i in range(HALVES)
        ]
        near = exchange(partial[HALVES * half :])
        next_t, *near = lax.optimization_barrier((next_t, *near))
        next_kv = jnp.transpose(next_t, (1, 0, 2))
        branch = finish(near, arrived, gate_row)
        return (branch, next_kv)

    return shards


def solution(mesh):
    return jax.shard_map(
        build(mesh.shape["head"], mesh.shape["patch"]),
        mesh=mesh,
        in_specs=(
            P(("groups", "patch", "head"), None, None),
            P(("groups", "patch"), None, "head"),
            P("head", None),
            P(),
            P("groups"),
            P("groups"),
        ),
        out_specs=(P(("groups", "patch", "head"), None), P(("groups", "patch"), None, "head")),
        check_vma=False,
    )
```

time: 37.5 us -> 36.4 us (0.971)
  waiting for transfers between devices: 12.7 us -> 7.44 us
  starting transfers between devices: 13.6 us -> 18 us
  other arithmetic: 1.73 us -> 0.97 us
  Pallas kernels: 3.59 us -> 4.17 us
    ppermute x1, waiting for transfers between devices: 6.7 us -> 0.78 us  [shards(): key_two = lax.ppermute(key_before, 'patch', onward)]
    ppermute x1, starting transfers between devices: 1.97 us -> 6 us  [shards(): value_two = lax.ppermute(value_before, 'patch', onward)]
    convert_element_type x1 -> x0, other arithmetic: 0.76 us -> none  [shards(): branch = (gate_row[None, :] * projected).astype(jnp.bfloat16)]
    ppermute x4 -> x6, starting transfers between devices: 2.54 us -> 3.14 us  [the longest x2 2.16 us: shards(): lax.ppermute(add_pair(*exchange(partial[i * half:(i + 1) * half])), 'head...]
    ppermute x1, waiting for transfers between devices: 0.01 us -> 0.59 us  [shards(): key_before = lax.ppermute(stale[:1], 'patch', onward)]
    pallas_call x2 -> x3, Pallas kernels: 3.46 us -> 4.05 us  [the longest x1 2.35 us: weigh(): pl.pallas_call(kernel, out_shape=[jax.ShapeDtypeStruct((heads, rows, late...]
    ppermute x1, waiting for transfers between devices: 1 us -> 1.52 us  [shards(): value_before = lax.ppermute(stale[1:], 'patch', onward)]
    ppermute x4 -> x6, waiting for transfers between devices: 4.34 us -> 4.21 us  [the longest x2 3.5 us: shards(): lax.ppermute(add_pair(*exchange(partial[i * half:(i + 1) * half])), 'head...]
  transfers between devices with their start and end apart: 11 -> 13, of which waited for: 6 -> 7; matrix products, arithmetic and copies ran while one was open for 8% -> 8% of each run, Pallas kernels for 7% -> 7%
where the time goes in v4:
time: 36.4 us; the launch traced here: 36.1 us
  starting transfers between devices  18 us (49%)
  waiting for transfers between devices  7.44 us (20%)
  Pallas kernels  4.17 us (11%)
  local copies, waits for them, and re-layouts  4.14 us (11%)
  between operations  1.39 us (4%)
  other arithmetic  0.97 us (3%)
    ppermute x1, starting transfers between devices, shards(): value_two = lax.ppermute(value_before, 'patch', onward)  6 us
    ppermute x2, waiting for transfers between devices, shards(): lax.ppermute(add_pair(*exchange(partial[i * half:(i + 1) * half])), 'head...  3.5 us
    ppermute x1, starting transfers between devices, shards(): key_before = lax.ppermute(stale[:1], 'patch', onward)  3.08 us
    ppermute x1, starting transfers between devices, shards(): value_before = lax.ppermute(stale[1:], 'patch', onward)  2.64 us
    pallas_call x1, Pallas kernels, weigh(): pl.pallas_call(kernel, out_shape=[jax.ShapeDtypeStruct((heads, rows, late...  2.35 us
    unnamed x6, local copies, waits for them, and re-layouts  2.25 us
    ppermute x2, starting transfers between devices, shards(): lax.ppermute(add_pair(*exchange(partial[i * half:(i + 1) * half])), 'head...  2.16 us
    ppermute x1, starting transfers between devices, shards(): key_two = lax.ppermute(key_before, 'patch', onward)  1.61 us
  transfers between devices with their start and end apart: 13, of which 7 were waited for; matrix products, arithmetic and copies ran while one was open for 8% of the time, Pallas kernels for 7%

profile of v4, /device:TPU:0, one launch (start us, length us, event | category | flops | bytes accessed | tf_op | source)
XLA Modules:
  0.0 36.1 jit_solution(5087950375957807311)
XLA Ops:
  0.6 1.2 %slice.9 = bf16[96,2,768]{2,1,0:T(2,128)(2,1)S(1)} slice(bf16[128,2,768]{2,1,0:T(2,128)(2,1)} %param.8), slice={[0:96], [0:2], [0:768]} | slice | bytes 589824 | tf_op jit(solution)/shard_map/slice | solution.py:250
  1.9 3.1 %collective-permute-start.1 = (bf16[1,96,768]{2,1,0:T(8,128)(2,1)S(1)}, bf16[1,96,768]{2,1,0:T(8,128)(2,1)S(1)}, u32[]{:S(2)}, u32[]{:S(2)}) collective-permute-start(bf16[1,96,768]{2,1,0:T(8,128)(2,1)S(1)} %get-tuple-element.55), channel_id=1, source_target_pairs={{0,4},{4,12},{12,8},{8,0},{1,5},{5,13},{13,9},{9,1},{2,6},{6,14},{... | collective-permute-start | bytes 442376 | tf_op jit(solution)/shard_map/ppermute | solution.py:255
  4.9 0.0 copy-start
  4.9 1.1 %copy-done = bf16[32,3,3072]{2,0,1:T(8,128)(2,1)S(1)} copy-done((bf16[32,3,3072]{2,0,1:T(8,128)(2,1)S(1)}, bf16[32,3,3072]{2,0,1:T(8,128)(2,1)}, u32[]{:S(2)}) %copy-start) | copy-done | bytes 589848
  6.0 0.1 shard_map.86
  6.1 0.1 collective-permute-start
  6.2 2.6 %collective-permute-start.6 = (bf16[1,96,768]{2,1,0:T(8,128)(2,1)S(1)}, bf16[1,96,768]{2,1,0:T(8,128)(2,1)S(1)}, u32[]{:S(2)}, u32[]{:S(2)}) collective-permute-start(bf16[1,96,768]{2,1,0:T(8,128)(2,1)S(1)} %get-tuple-element.54), channel_id=1, source_target_pairs={{0,4},{4,12},{12,8},{8,0},{1,5},{5,13},{13,9},{9,1},{2,6},{6,14},{... | collective-permute-start | bytes 442376 | tf_op jit(solution)/shard_map/ppermute | solution.py:256
  8.9 0.3 collective-permute-start.4
  9.2 0.6 %collective-permute-done.1.rest_4_ = bf16[1,96,768]{2,1,0:T(8,128)(2,1)S(1)} collective-permute-done((bf16[1,96,768]{2,1,0:T(8,128)(2,1)S(1)}, bf16[1,96,768]{2,1,0:T(8,128)(2,1)S(1)}, u32[]{:S(2)}, u32[]{:S(2)}) %collective-permute-start.1) | collective-permute-done | bytes 147488 | tf_op jit(solution)/shard_map/ppermute | solution.py:255
  9.8 1.6 %collective-permute-start.5 = (bf16[1,96,768]{2,1,0:T(8,128)(2,1)S(1)}, bf16[1,96,768]{2,1,0:T(8,128)(2,1)S(1)}, u32[]{:S(2)}, u32[]{:S(2)}) collective-permute-start(bf16[1,96,768]{2,1,0:T(8,128)(2,1)S(1)} %collective-permute-done.1.rest_4_), channel_id=1, source_target_pairs={{0,4},{4,12},{12,8},{8,0},{1,5},{5,13},{13,9},{9,1},{2,6},{6,14},{... | collective-permute-start | bytes 442376 | tf_op jit(solution)/shard_map/ppermute | solution.py:260
  11.4 1.5 %collective-permute-start.2 = (bf16[3,32,768]{2,1,0:T(8,128)(2,1)S(1)}, bf16[3,32,768]{2,1,0:T(8,128)(2,1)S(1)}, u32[]{:S(2)}, u32[]{:S(2)}) collective-permute-start(bf16[3,32,768]{2,1,0:T(8,128)(2,1)S(1)} %get-tuple-element.32), channel_id=1, source_target_pairs={{0,2},{1,3},{2,0},{3,1},{4,6},{5,7},{6,4},{7,5},{8,10},{9,11},{10,... | collective-permute-start | bytes 442376 | tf_op jit(solution)/shard_map/ppermute | solution.py:267
  12.9 0.0 collective-permute-done.rest_1_
  12.9 0.0 collective-permute-start.3
  12.9 1.5 %collective-permute-done.6.rest_7_ = bf16[1,96,768]{2,1,0:T(8,128)(2,1)S(1)} collective-permute-done((bf16[1,96,768]{2,1,0:T(8,128)(2,1)S(1)}, bf16[1,96,768]{2,1,0:T(8,128)(2,1)S(1)}, u32[]{:S(2)}, u32[]{:S(2)}) %collective-permute-start.6) | collective-permute-done | bytes 147488 | tf_op jit(solution)/shard_map/ppermute | solution.py:256
  14.4 6.0 %collective-permute-start.7 = (bf16[1,96,768]{2,1,0:T(8,128)(2,1)S(1)}, bf16[1,96,768]{2,1,0:T(8,128)(2,1)S(1)}, u32[]{:S(2)}, u32[]{:S(2)}) collective-permute-start(bf16[1,96,768]{2,1,0:T(8,128)(2,1)S(1)} %collective-permute-done.6.rest_7_), channel_id=1, source_target_pairs={{0,4},{4,12},{12,8},{8,0},{1,5},{5,13},{13,9},{9,1},{2,6},{6,14},{... | collective-permute-start | bytes 442376 | tf_op jit(solution)/shard_map/ppermute | solution.py:261
  20.4 0.7 %constant_dynamic-slice_fusion = s32[1,512]{1,0:T(1,128)S(1)} fusion(s32[4,512]{1,0:T(4,128)} %constant.34.clone, u32[]{:T(128)S(6)} %convert_element_type.28), kind=kLoop, calls=%fused_computation.13 | loop fusion | bytes 4100 | tf_op jit(solution)/shard_map/dynamic_slice | solution.py:236
  21.8 0.7 %convert_reduce_fusion = s32[512]{0:T(512)S(1)} fusion(s32[512]{0:T(512)S(1)} %fusion.2, s32[512]{0:T(512)S(1)} %bitcast.16, s32[4]{0:T(128)} %param.11), kind=kLoop, calls=%fused_computation.4 | loop fusion | flops 9728 | bytes 6160 | tf_op jit(solution)/shard_map/reduce_sum | solution.py:245
  22.5 0.8 %collective-permute-done.5.rest_6_ = bf16[1,96,768]{2,1,0:T(8,128)(2,1)S(1)} collective-permute-done((bf16[1,96,768]{2,1,0:T(8,128)(2,1)S(1)}, bf16[1,96,768]{2,1,0:T(8,128)(2,1)S(1)}, u32[]{:S(2)}, u32[]{:S(2)}) %collective-permute-start.5) | collective-permute-done | bytes 147488 | tf_op jit(solution)/shard_map/ppermute | solution.py:260
  23.3 0.0 collective-permute-done.2.rest_2_
  23.3 0.0 collective-permute-done.3.rest_3_
  23.3 0.0 collective-permute-done.4.rest_5_.rest_8_
  23.3 2.4 %shard_map.87 = (bf16[6,128,128]{2,1,0:T(8,128)(2,1)S(1)}, f32[128,768]{1,0:T(8,128)S(1)}, f32[6,128,1]{2,1,0:T(8,128)S(1)}, bf16[2,128,768]{2,1,0:T(8,128)(2,1)S(1)}, bf16[768,3072]{1,0:T(8,128)(2,1)S(1)}) custom-call(s32[1,512]{1,0:T(1,128)S(1)} %bitcast.13, bf16[3,32,768]{2,1,0:T(8,128)(2,1)S(1)} %get-tuple-element.27.rest_0_, ...), custom_call_target="tpu_custom_call" | custom-call | tf_op jit(solution)/shard_map/pallas_call | solution.py:128
  25.7 0.0 copy-start.1
  25.7 0.3 collective-permute-done.7.rest_0_
  26.0 0.9 %shard_map.88 = (bf16[16,3072]{1,0:T(8,128)(2,1)S(1)}, bf16[16,3072]{1,0:T(8,128)(2,1)S(1)}, bf16[16,3072]{1,0:T(8,128)(2,1)S(1)}, bf16[16,3072]{1,0:T(8,128)(2,...) custom-call(bf16[6,128,128]{2,1,0:T(8,128)(2,1)S(1)} %get-tuple-element.37.weights_ref, ...), custom_call_target="tpu_custom_call" | custom-call | tf_op jit(solution)/shard_map/pallas_call | solution.py:179
  27.0 0.1 collective-permute-start.11
  27.0 0.5 %collective-permute-start.9 = (bf16[16,3072]{1,0:T(8,128)(2,1)S(1)}, bf16[16,3072]{1,0:T(8,128)(2,1)S(1)}, u32[]{:S(2)}, u32[]{:S(2)}) collective-permute-start(bf16[16,3072]{1,0:T(8,128)(2,1)S(1)} %get-tuple-element.46), channel_id=1, source_target_pairs={{0,1},{1,0},{2,3},{3,2},{4,5},{5,4},{6,7},{7,6},{8,9},{9,8},{10,11... | collective-permute-start | bytes 294920 | tf_op jit(solution)/shard_map/ppermute | solution.py:278
  27.5 0.1 collective-permute-start.8
  27.6 0.7 %collective-permute-done.11 = bf16[16,3072]{1,0:T(8,128)(2,1)S(1)} collective-permute-done((bf16[16,3072]{1,0:T(8,128)(2,1)S(1)}, bf16[16,3072]{1,0:T(8,128)(2,1)S(1)}, u32[]{:S(2)}, u32[]{:S(2)}) %collective-permute-start.11) | collective-permute-done | bytes 98336 | tf_op jit(solution)/shard_map/ppermute | solution.py:278
  28.4 1.6 %collective-permute-start.12 = (bf16[16,3072]{1,0:T(8,128)(2,1)S(1)}, bf16[16,3072]{1,0:T(8,128)(2,1)S(1)}, u32[]{:S(2)}, u32[]{:S(2)}) collective-permute-start(bf16[16,3072]{1,0:T(8,128)(2,1)S(1)} %add_convert_fusion), channel_id=1, source_target_pairs={{0,2},{1,3},{2,0},{3,1},{4,6},{5,7},{6,4},{7,5},{8,10},{9,11},{10,... | collective-permute-start | bytes 294920 | tf_op jit(solution)/shard_map/ppermute | solution.py:295
  29.9 0.0 collective-permute-done.9
  30.0 0.6 %collective-permute-start.10 = (bf16[16,3072]{1,0:T(8,128)(2,1)S(1)}, bf16[16,3072]{1,0:T(8,128)(2,1)S(1)}, u32[]{:S(2)}, u32[]{:S(2)}) collective-permute-start(bf16[16,3072]{1,0:T(8,128)(2,1)S(1)} %add_convert_fusion.1), channel_id=1, source_target_pairs={{0,2},{1,3},{2,0},{3,1},{4,6},{5,7},{6,4},{7,5},{8,10},{9,11},{10,... | collective-permute-start | bytes 294920 | tf_op jit(solution)/shard_map/ppermute | solution.py:295
  30.5 0.0 copy-done.1
  30.6 0.2 select_reduce_fusion
  30.7 0.0 collective-permute-done.8.rest_1_
  30.7 1.2 %copy.12 = bf16[128,2,768]{2,1,0:T(2,128)(2,1)} copy(bf16[128,2,768]{2,0,1:T(8,128)(2,1)S(1)} %bitcast.11) | data formatting | bytes 786432
  31.9 2.2 %collective-permute-done.12.rest_3_ = bf16[16,3072]{1,0:T(8,128)(2,1)S(1)} collective-permute-done((bf16[16,3072]{1,0:T(8,128)(2,1)S(1)}, bf16[16,3072]{1,0:T(8,128)(2,1)S(1)}, u32[]{:S(2)}, u32[]{:S(2)}) %collective-permute-start.12) | collective-permute-done | bytes 98336 | tf_op jit(solution)/shard_map/ppermute | solution.py:295
  34.1 1.3 %collective-permute-done.10.rest_2_ = bf16[16,3072]{1,0:T(8,128)(2,1)S(1)} collective-permute-done((bf16[16,3072]{1,0:T(8,128)(2,1)S(1)}, bf16[16,3072]{1,0:T(8,128)(2,1)S(1)}, u32[]{:S(2)}, u32[]{:S(2)}) %collective-permute-start.10) | collective-permute-done | bytes 98336 | tf_op jit(solution)/shard_map/ppermute | solution.py:295
  35.4 0.8 %shard_map.89 = bf16[32,3072]{1,0:T(8,128)(2,1)} custom-call(f32[1,3072]{1,0:T(1,128)S(1)} %bitcast.12, bf16[32,3072]{1,0:T(8,128)(2,1)S(1)} %get-tuple-element.43.rest_0_, bf16[32,3072]{1,0:T(8,128)(2,1)S(1)} %collective-permute-done.8.rest_1_, bf16[16,3072]{1,0:T(8,128)(2,1)S(1)} %collective-permute-done.10.rest_2_, ...), custom_call_target="tpu_custom_call" | custom-call | tf_op jit(solution)/shard_map/pallas_call | solution.py:201
  (6 shorter events, 0.1 us)
Async XLA Ops:
  1.9 7.9 %collective-permute-start.1 = (bf16[1,96,768]{2,1,0:T(8,128)(2,1)S(1)}, bf16[1,96,768]{2,1,0:T(8,128)(2,1)S(1)}, u32[]{:S(2)}, u32[]{:S(2)}) collective-permute-start(bf16[1,96,768]{2,1,0:T(8,128)(2,1)S(1)} %get-tuple-element.55), channel_id=1, source_target_pairs={{0,4},{4,12},{12,8},{8,0},{1,5},{5,13},{13,9},{9,1},{2,6},{6,14},{... | collective-permute-start | bytes 442376 | tf_op jit(solution)/shard_map/ppermute | solution.py:255
  4.9 1.1 %copy-start = (bf16[32,3,3072]{2,0,1:T(8,128)(2,1)S(1)}, bf16[32,3,3072]{2,0,1:T(8,128)(2,1)}, u32[]{:S(2)}) copy-start(bf16[32,3,3072]{2,0,1:T(8,128)(2,1)} %param.7) | copy-start | bytes 1769476
  6.1 6.8 %collective-permute-start = (bf16[3,32,768]{2,1,0:T(8,128)(2,1)S(1)}, bf16[3,32,768]{2,1,0:T(8,128)(2,1)S(1)}, u32[]{:S(2)}, u32[]{:S(2)}) collective-permute-start(bf16[3,32,768]{2,1,0:T(8,128)(2,1)S(1)} %get-tuple-element.28), channel_id=1, source_target_pairs={{0,1},{1,0},{2,3},{3,2},{4,5},{5,4},{6,7},{7,6},{8,9},{9,8},{10,11... | collective-permute-start | bytes 442376 | tf_op jit(solution)/shard_map/ppermute | solution.py:267
  6.2 8.2 %collective-permute-start.6 = (bf16[1,96,768]{2,1,0:T(8,128)(2,1)S(1)}, bf16[1,96,768]{2,1,0:T(8,128)(2,1)S(1)}, u32[]{:S(2)}, u32[]{:S(2)}) collective-permute-start(bf16[1,96,768]{2,1,0:T(8,128)(2,1)S(1)} %get-tuple-element.54), channel_id=1, source_target_pairs={{0,4},{4,12},{12,8},{8,0},{1,5},{5,13},{13,9},{9,1},{2,6},{6,14},{... | collective-permute-start | bytes 442376 | tf_op jit(solution)/shard_map/ppermute | solution.py:256
  8.9 14.5 %collective-permute-start.4 = (bf16[2,96,768]{2,1,0:T(8,128)(2,1)S(1)}, bf16[2,96,768]{2,1,0:T(8,128)(2,1)S(1)}, u32[]{:S(2)}, u32[]{:S(2)}) collective-permute-start(bf16[2,96,768]{2,1,0:T(8,128)(2,1)S(1)} %bitcast.15), channel_id=1, source_target_pairs={{4,0},{12,4},{8,12},{0,8},{5,1},{13,5},{9,13},{1,9},{6,2},{14,6},{... | collective-permute-start | bytes 884744 | tf_op jit(solution)/shard_map/ppermute | solution.py:259
  9.8 13.5 %collective-permute-start.5 = (bf16[1,96,768]{2,1,0:T(8,128)(2,1)S(1)}, bf16[1,96,768]{2,1,0:T(8,128)(2,1)S(1)}, u32[]{:S(2)}, u32[]{:S(2)}) collective-permute-start(bf16[1,96,768]{2,1,0:T(8,128)(2,1)S(1)} %collective-permute-done.1.rest_4_), channel_id=1, source_target_pairs={{0,4},{4,12},{12,8},{8,0},{1,5},{5,13},{13,9},{9,1},{2,6},{6,14},{... | collective-permute-start | bytes 442376 | tf_op jit(solution)/shard_map/ppermute | solution.py:260
  11.4 11.9 %collective-permute-start.2 = (bf16[3,32,768]{2,1,0:T(8,128)(2,1)S(1)}, bf16[3,32,768]{2,1,0:T(8,128)(2,1)S(1)}, u32[]{:S(2)}, u32[]{:S(2)}) collective-permute-start(bf16[3,32,768]{2,1,0:T(8,128)(2,1)S(1)} %get-tuple-element.32), channel_id=1, source_target_pairs={{0,2},{1,3},{2,0},{3,1},{4,6},{5,7},{6,4},{7,5},{8,10},{9,11},{10,... | collective-permute-start | bytes 442376 | tf_op jit(solution)/shard_map/ppermute | solution.py:267
  12.9 10.4 %collective-permute-start.3 = (bf16[3,32,768]{2,1,0:T(8,128)(2,1)S(1)}, bf16[3,32,768]{2,1,0:T(8,128)(2,1)S(1)}, u32[]{:S(2)}, u32[]{:S(2)}) collective-permute-start(bf16[3,32,768]{2,1,0:T(8,128)(2,1)S(1)} %get-tuple-element.33), channel_id=1, source_target_pairs={{0,3},{1,2},{2,1},{3,0},{4,7},{5,6},{6,5},{7,4},{8,11},{9,10},{10,... | collective-permute-start | bytes 442376 | tf_op jit(solution)/shard_map/ppermute | solution.py:267
  14.4 11.6 %collective-permute-start.7 = (bf16[1,96,768]{2,1,0:T(8,128)(2,1)S(1)}, bf16[1,96,768]{2,1,0:T(8,128)(2,1)S(1)}, u32[]{:S(2)}, u32[]{:S(2)}) collective-permute-start(bf16[1,96,768]{2,1,0:T(8,128)(2,1)S(1)} %collective-permute-done.6.rest_7_), channel_id=1, source_target_pairs={{0,4},{4,12},{12,8},{8,0},{1,5},{5,13},{13,9},{9,1},{2,6},{6,14},{... | collective-permute-start | bytes 442376 | tf_op jit(solution)/shard_map/ppermute | solution.py:261
  25.7 4.9 %copy-start.1 = (bf16[50,3072]{1,0:T(8,128)(2,1)S(1)}, bf16[50,3072]{1,0:T(8,128)(2,1)}, u32[]{:S(2)}) copy-start(bf16[50,3072]{1,0:T(8,128)(2,1)} %param.10) | copy-start | bytes 921604
  27.0 1.4 %collective-permute-start.11 = (bf16[16,3072]{1,0:T(8,128)(2,1)S(1)}, bf16[16,3072]{1,0:T(8,128)(2,1)S(1)}, u32[]{:S(2)}, u32[]{:S(2)}) collective-permute-start(bf16[16,3072]{1,0:T(8,128)(2,1)S(1)} %get-tuple-element.48), channel_id=1, source_target_pairs={{0,1},{1,0},{2,3},{3,2},{4,5},{5,4},{6,7},{7,6},{8,9},{9,8},{10,11... | collective-permute-start | bytes 294920 | tf_op jit(solution)/shard_map/ppermute | solution.py:278
  27.0 2.9 %collective-permute-start.9 = (bf16[16,3072]{1,0:T(8,128)(2,1)S(1)}, bf16[16,3072]{1,0:T(8,128)(2,1)S(1)}, u32[]{:S(2)}, u32[]{:S(2)}) collective-permute-start(bf16[16,3072]{1,0:T(8,128)(2,1)S(1)} %get-tuple-element.46), channel_id=1, source_target_pairs={{0,1},{1,0},{2,3},{3,2},{4,5},{5,4},{6,7},{7,6},{8,9},{9,8},{10,11... | collective-permute-start | bytes 294920 | tf_op jit(solution)/shard_map/ppermute | solution.py:278
  27.5 3.2 %collective-permute-start.8 = (bf16[32,3072]{1,0:T(8,128)(2,1)S(1)}, bf16[32,3072]{1,0:T(8,128)(2,1)S(1)}, u32[]{:S(2)}, u32[]{:S(2)}) collective-permute-start(bf16[32,3072]{1,0:T(8,128)(2,1)S(1)} %get-tuple-element.42), channel_id=1, source_target_pairs={{0,1},{1,0},{2,3},{3,2},{4,5},{5,4},{6,7},{7,6},{8,9},{9,8},{10,11... | collective-permute-start | bytes 589832 | tf_op jit(solution)/shard_map/ppermute | solution.py:278
  28.4 5.7 %collective-permute-start.12 = (bf16[16,3072]{1,0:T(8,128)(2,1)S(1)}, bf16[16,3072]{1,0:T(8,128)(2,1)S(1)}, u32[]{:S(2)}, u32[]{:S(2)}) collective-permute-start(bf16[16,3072]{1,0:T(8,128)(2,1)S(1)} %add_convert_fusion), channel_id=1, source_target_pairs={{0,2},{1,3},{2,0},{3,1},{4,6},{5,7},{6,4},{7,5},{8,10},{9,11},{10,... | collective-permute-start | bytes 294920 | tf_op jit(solution)/shard_map/ppermute | solution.py:295
  30.0 5.4 %collective-permute-start.10 = (bf16[16,3072]{1,0:T(8,128)(2,1)S(1)}, bf16[16,3072]{1,0:T(8,128)(2,1)S(1)}, u32[]{:S(2)}, u32[]{:S(2)}) collective-permute-start(bf16[16,3072]{1,0:T(8,128)(2,1)S(1)} %add_convert_fusion.1), channel_id=1, source_target_pairs={{0,2},{1,3},{2,0},{3,1},{4,6},{5,7},{6,4},{7,5},{8,10},{9,11},{10,... | collective-permute-start | bytes 294920 | tf_op jit(solution)/shard_map/ppermute | solution.py:295
